TPU v7x, 32 devices: a whole 2x2x4 slice. The times are simulated.
32 devices in a mesh: view: 2 (over y), scene: 16 (over z, x, core).
Axes of the slice: x: 2, y: 2, z: 4, core: 2. Of those that a mesh axis runs over, the one named last changes fastest.
Arguments:
- means: float32 [64, 3, 128], P(('view', 'scene')), may hold values from -3 to 3
- log_scales: float32 [64, 3, 128], P(('view', 'scene')), may hold values from -3.3 to -0.4, as said below
- rotations: float32 [64, 4, 128], P(('view', 'scene')), may hold values from -2.5 to 2.5
- opacity_logits: float32 [64, 1, 128], P(('view', 'scene')), may hold values from -3 to 3
- colour_coefs: float32 [64, 48, 128], P(('view', 'scene')), may hold values from -2 to 2
- cameras: float32 [2, 16], replicated, may hold values from -1 to 2048, as said below
- exposure: float32 [2, 12], P('view'), may hold values from -1 to 1
- target: float32 [2, 256, 3, 256], P('view', 'scene'), may hold values from 0 to 1
- tile_ids: int32 [2, 256], P('view', 'scene'), may hold values from 0 to 255, each once within a row
- send_list: int32 [2, 16, 16, 2], P('view', 'scene'), may hold values from -1 to 3, as said below
- pair_slots: int32 [2, 256, 4], P('view', 'scene'), may hold values from -1 to 31, as said below
Outputs:
- shown: float32 [2, 256, 3, 256], P('view', 'scene')
- grad_means: float32 [64, 3, 128], P(('view', 'scene'))
- grad_log_scales: float32 [64, 3, 128], P(('view', 'scene'))
- grad_rotations: float32 [64, 4, 128], P(('view', 'scene'))
- grad_opacity: float32 [64, 1, 128], P(('view', 'scene'))
- grad_colour: float32 [64, 48, 128], P(('view', 'scene'))
- grad_exposure: float32 [2, 12], P('view')
Inputs may be any that keep to these rules, and one draw needn't show every extreme that they name: send_list[v, s, r, c] is a local block number of owner s or -1; in each row of 2 the live entries come first and are all different, and a row may have none; in every image some renderer gets 2 blocks from every owner. pair_slots[v, t, k] is -1 or s * 2 + c with c below the number of live entries of send_list[v, s, t // 16]; a tile's live entries come first, at least one, all different; in every image each renderer has a tile with 4 live entries. `cameras`: each row is a rotation matrix, a translation, two focal lengths and a principal point; every Gaussian lies at depth 4 or more before each camera. `log_scales`: logarithms of lengths in world units.
All inputs are finite; a program needn't handle non-finite values.
Results may differ from a plain program's by a relative error of at most 0.0003.
Values sent between devices are 32-bit elements; how exact they have to be, the bound alone decides.
A program may use at most 64 MiB of HBM per device.

v0:
```python
import jax
import jax.numpy as jnp
from jax import lax
from jax.sharding import PartitionSpec as P

PIX = 256
TILE_COLS = 32


SH_ZERO = 0.28209479177387814
SH_ONE = 0.4886025119029199
SH_TWO = (
    1.0925484305920792,
    -1.0925484305920792,
    0.31539156525252005,
    -1.0925484305920792,
    0.5462742152960396,
)
SH_THREE = (
    -0.5900435899266435,
    2.890611442640554,
    -0.4570457994644658,
    0.3731763325901154,
    -0.4570457994644658,
    1.445305721320277,
    -0.5900435899266435,
)


def harmonics(dir_x, dir_y, dir_z):
    sq_x, sq_y, sq_z = (dir_x * dir_x, dir_y * dir_y, dir_z * dir_z)
    sh_basis = [
        SH_ZERO * jnp.ones_like(dir_x),
        -SH_ONE * dir_y,
        SH_ONE * dir_z,
        -SH_ONE * dir_x,
        SH_TWO[0] * dir_x * dir_y,
        SH_TWO[1] * dir_y * dir_z,
        SH_TWO[2] * (2.0 * sq_z - sq_x - sq_y),
        SH_TWO[3] * dir_x * dir_z,
        SH_TWO[4] * (sq_x - sq_y),
        SH_THREE[0] * dir_y * (3.0 * sq_x - sq_y),
        SH_THREE[1] * dir_x * dir_y * dir_z,
        SH_THREE[2] * dir_y * (4.0 * sq_z - sq_x - sq_y),
        SH_THREE[3] * dir_z * (2.0 * sq_z - 3.0 * sq_x - 3.0 * sq_y),
        SH_THREE[4] * dir_x * (4.0 * sq_z - sq_x - sq_y),
        SH_THREE[5] * dir_z * (sq_x - sq_y),
        SH_THREE[6] * dir_x * (sq_x - 3.0 * sq_y),
    ]
    return jnp.stack(sh_basis, axis=1)


def project(pieces, camera):
    means, log_scales, rotations, opacity_logits, colour_coefs = pieces
    rotation = camera[0:9].reshape(3, 3)
    translation = camera[9:12]
    focal_x, focal_y, centre_x, centre_y = (camera[12], camera[13], camera[14], camera[15])
    position = [means[:, 0], means[:, 1], means[:, 2]]
    view_pos = [
        rotation[row_at, 0] * position[0]
        + rotation[row_at, 1] * position[1]
        + rotation[row_at, 2] * position[2]
        + translation[row_at]
        for row_at in range(3)
    ]
    inv_depth = 1.0 / view_pos[2]
    quat_w = rotations[:, 0] + 3.0
    quat_x, quat_y, quat_z = (rotations[:, 1], rotations[:, 2], rotations[:, 3])
    quat_norm = jnp.sqrt(quat_w * quat_w + quat_x * quat_x + quat_y * quat_y + quat_z * quat_z)
    quat_w, quat_x, quat_y, quat_z = (
        quat_w / quat_norm,
        quat_x / quat_norm,
        quat_y / quat_norm,
        quat_z / quat_norm,
    )
    spin_matrix = [
        [
            1.0 - 2.0 * (quat_y * quat_y + quat_z * quat_z),
            2.0 * (quat_x * quat_y - quat_w * quat_z),
            2.0 * (quat_x * quat_z + quat_w * quat_y),
        ],
        [
            2.0 * (quat_x * quat_y + quat_w * quat_z),
            1.0 - 2.0 * (quat_x * quat_x + quat_z * quat_z),
            2.0 * (quat_y * quat_z - quat_w * quat_x),
        ],
        [
            2.0 * (quat_x * quat_z - quat_w * quat_y),
            2.0 * (quat_y * quat_z + quat_w * quat_x),
            1.0 - 2.0 * (quat_x * quat_x + quat_y * quat_y),
        ],
    ]
    scales = jnp.exp(log_scales)
    world_frame = [
        [spin_matrix[row_at][col_at] * scales[:, col_at] for col_at in range(3)]
        for row_at in range(3)
    ]
    jacobian = [
        [
            focal_x * inv_depth * rotation[0, col_at]
            - focal_x * view_pos[0] * inv_depth * inv_depth * rotation[2, col_at]
            for col_at in range(3)
        ],
        [
            focal_y * inv_depth * rotation[1, col_at]
            - focal_y * view_pos[1] * inv_depth * inv_depth * rotation[2, col_at]
            for col_at in range(3)
        ],
    ]
    screen_frame = [
        [
            jacobian[row_at][0] * world_frame[0][col_at]
            + jacobian[row_at][1] * world_frame[1][col_at]
            + jacobian[row_at][2] * world_frame[2][col_at]
            for col_at in range(3)
        ]
        for row_at in range(2)
    ]
    sigma_xx = screen_frame[0][0] ** 2 + screen_frame[0][1] ** 2 + screen_frame[0][2] ** 2 + 0.3
    sigma_yy = screen_frame[1][0] ** 2 + screen_frame[1][1] ** 2 + screen_frame[1][2] ** 2 + 0.3
    sigma_xy = (
        screen_frame[0][0] * screen_frame[1][0]
        + screen_frame[0][1] * screen_frame[1][1]
        + screen_frame[0][2] * screen_frame[1][2]
    )
    determinant = sigma_xx * sigma_yy - sigma_xy * sigma_xy
    screen_x = focal_x * view_pos[0] * inv_depth + centre_x
    screen_y = focal_y * view_pos[1] * inv_depth + centre_y
    opacity = jax.nn.sigmoid(opacity_logits[:, 0])
    eye_pos = [
        -(
            rotation[0, col_at] * translation[0]
            + rotation[1, col_at] * translation[1]
            + rotation[2, col_at] * translation[2]
        )
        for col_at in range(3)
    ]
    offsets = [position[col_at] - eye_pos[col_at] for col_at in range(3)]
    eye_dist = jnp.sqrt(offsets[0] ** 2 + offsets[1] ** 2 + offsets[2] ** 2)
    sh_basis = harmonics(offsets[0] / eye_dist, offsets[1] / eye_dist, offsets[2] / eye_dist)
    sh_coefs = colour_coefs.reshape(colour_coefs.shape[0], 16, 3, colour_coefs.shape[2])
    colour = jnp.maximum(0.5 + jnp.sum(sh_basis[:, :, None, :] * sh_coefs, axis=1), 0.0)
    shape_rows = jnp.stack(
        [
            screen_x,
            screen_y,
            sigma_yy / determinant,
            -sigma_xy / determinant,
            sigma_xx / determinant,
            opacity,
        ],
        axis=1,
    )
    return jnp.concatenate([shape_rows, colour], axis=1)


def composite(chosen_blk, live_mask, tile_id):
    lane_count = chosen_blk.shape[2]
    pixel_index = jnp.arange(PIX, dtype=jnp.int32)
    pixel_x = (16 * (tile_id % TILE_COLS) + pixel_index % 16).astype(jnp.float32) + 0.5
    pixel_y = (16 * (tile_id // TILE_COLS) + pixel_index // 16).astype(jnp.float32) + 0.5
    gap_x = pixel_x[None, :, None] - chosen_blk[:, 0][:, None, :]
    gap_y = pixel_y[None, :, None] - chosen_blk[:, 1][:, None, :]
    falloff = (
        0.5
        * (
            chosen_blk[:, 2][:, None, :] * gap_x * gap_x
            + chosen_blk[:, 4][:, None, :] * gap_y * gap_y
        )
        + chosen_blk[:, 3][:, None, :] * gap_x * gap_y
    )
    alpha_vals = (
        chosen_blk[:, 5][:, None, :]
        * jnp.exp(-falloff)
        * live_mask.astype(jnp.float32)[:, None, None]
    )
    log_keep = jnp.log1p(-alpha_vals)
    lane_index = jnp.arange(lane_count)
    strict = (lane_index[:, None] < lane_index[None, :]).astype(jnp.float32)
    inside = jnp.dot(
        log_keep.reshape(-1, lane_count), strict, precision=lax.Precision.HIGHEST
    ).reshape(log_keep.shape)
    totals = jnp.sum(log_keep, axis=2)
    before = jnp.cumsum(totals, axis=0) - totals
    transmit = jnp.exp(inside + before[:, :, None])
    return jnp.einsum(
        "kpg,kcg->cp", alpha_vals * transmit, chosen_blk[:, 6:9], precision=lax.Precision.HIGHEST
    )


def local(
    means,
    log_scales,
    rotations,
    opacity_logits,
    colour_coefs,
    cameras,
    exposure,
    target,
    tile_ids,
    send_list,
    pair_slots,
):
    view_count = lax.axis_size("view")
    scene_count = lax.axis_size("scene")
    own_params = (means, log_scales, rotations, opacity_logits, colour_coefs)
    per_device = means.shape[0]
    owned_count = per_device * view_count
    feature_count = 9
    lane_count = means.shape[2]
    capacity = send_list.shape[3]
    own_proj, unproject = jax.vjp(
        lambda *pieces: jax.vmap(lambda cam_row: project(pieces, cam_row))(cameras), *own_params
    )
    arrived = lax.all_to_all(own_proj, "view", split_axis=0, concat_axis=0, tiled=True)
    projected = arrived.reshape(owned_count, feature_count, lane_count)
    send_picks = send_list[0, 0]
    outgoing = jnp.take(projected, jnp.maximum(send_picks, 0).reshape(-1), axis=0)
    outgoing = (
        outgoing.reshape(scene_count, capacity, feature_count, lane_count)
        * (send_picks >= 0).astype(jnp.float32)[:, :, None, None]
    )
    incoming = lax.all_to_all(outgoing, "scene", split_axis=0, concat_axis=0, tiled=True).reshape(
        scene_count * capacity, feature_count, lane_count
    )
    mixing = jnp.eye(3, dtype=jnp.float32) + exposure[0, 0:9].reshape(3, 3)
    offset = exposure[0, 9:12]

    def render_tile(tile_items):
        tile_id, slot_list, goal_tile = tile_items
        live_mask = slot_list >= 0
        chosen = jnp.take(incoming, jnp.maximum(slot_list, 0), axis=0)
        colour, shade_back = jax.vjp(
            lambda chosen_blk: composite(chosen_blk, live_mask, tile_id), chosen
        )
        shown_tile = jnp.dot(mixing, colour, precision=lax.Precision.HIGHEST) + offset[:, None]
        miss_tile = shown_tile - goal_tile
        grad_chosen = shade_back(jnp.dot(mixing.T, miss_tile, precision=lax.Precision.HIGHEST))[0]
        expo_terms = jnp.concatenate(
            [
                jnp.dot(miss_tile, colour.T, precision=lax.Precision.HIGHEST).reshape(9),
                jnp.sum(miss_tile, axis=1),
            ]
        )
        return (shown_tile, grad_chosen, expo_terms)

    shown_tiles, grad_chosen, expo_terms = lax.map(
        render_tile, (tile_ids[0], pair_slots[0], target[0])
    )
    dump_index = scene_count * capacity
    where_to = jnp.where(pair_slots[0] >= 0, pair_slots[0], dump_index).reshape(-1)
    grad_incoming = (
        jnp.zeros((dump_index, feature_count, lane_count), jnp.float32)
        .at[where_to]
        .add(grad_chosen.reshape(-1, feature_count, lane_count), mode="drop")
    )
    returned = lax.all_to_all(
        grad_incoming.reshape(scene_count, capacity, feature_count, lane_count),
        "scene",
        split_axis=0,
        concat_axis=0,
        tiled=True,
    )
    home_index = jnp.where(send_picks >= 0, send_picks, owned_count).reshape(-1)
    grad_projected = (
        jnp.zeros((owned_count, feature_count, lane_count), jnp.float32)
        .at[home_index]
        .add(returned.reshape(-1, feature_count, lane_count), mode="drop")
    )
    sent_back = lax.all_to_all(
        grad_projected.reshape(view_count, per_device, feature_count, lane_count),
        "view",
        split_axis=0,
        concat_axis=0,
        tiled=True,
    )
    param_grads = unproject(sent_back)
    exposure_grad = lax.psum(jnp.sum(expo_terms, axis=0), "scene")
    return (
        shown_tiles[None],
        param_grads[0],
        param_grads[1],
        param_grads[2],
        param_grads[3],
        param_grads[4],
        exposure_grad[None],
    )


def solution(mesh):
    return jax.shard_map(
        local,
        mesh=mesh,
        in_specs=(
            P(("view", "scene"), None, None),
            P(("view", "scene"), None, None),
            P(("view", "scene"), None, None),
            P(("view", "scene"), None, None),
            P(("view", "scene"), None, None),
            P(),
            P("view", None),
            P("view", "scene", None, None),
            P("view", "scene"),
            P("view", "scene", None, None),
            P("view", "scene", None),
        ),
        out_specs=(
            P("view", "scene", None, None),
            P(("view", "scene"), None, None),
            P(("view", "scene"), None, None),
            P(("view", "scene"), None, None),
            P(("view", "scene"), None, None),
            P(("view", "scene"), None, None),
            P("view", None),
        ),
        check_vma=False,
    )
```

profile of v0, /device:TPU:0, one launch (start us, length us, event | category | flops | bytes accessed | tf_op | source)
XLA Modules:
  0.0 258.7 jit_solution(15087173958095727536)
XLA Ops:
  7.0 4.4 %all-to-all-start = ((f32[2,2,9,128]{3,1,2,0:T(2,128)}), f32[2,2,9,128]{3,1,2,0:T(2,128)S(1)}, u32[]{:S(2)}, u32[]{:S(2)}) async-start(f32[2,2,9,128]{3,1,2,0:T(2,128)} %copy.793), calls=%async_computation | async-start | bytes 36864 | tf_op jit(solution)/shard_map/all_to_all | solution.py:215
  12.5 2.7 %all-to-all-done = f32[2,2,9,128]{3,1,2,0:T(2,128)S(1)} async-done(((f32[2,2,9,128]{3,1,2,0:T(2,128)}), f32[2,2,9,128]{3,1,2,0:T(2,128)S(1)}, u32[]{:S(2)}, u32[]{:S(2)}) %all-to-all-start) | async-done | bytes 18464 | tf_op jit(solution)/shard_map/all_to_all | solution.py:215
  16.7 6.5 %all-to-all-start.1 = ((f32[16,2,9,128]{3,1,2,0:T(2,128)}), f32[16,2,9,128]{3,1,2,0:T(2,128)S(1)}, u32[]{:S(2)}, u32[]{:S(2)}) async-start(f32[16,2,9,128]{3,1,2,0:T(2,128)} %fusion.49), calls=%async_computation.1 | async-start | bytes 294912 | tf_op jit(solution)/shard_map/all_to_all | solution.py:223
  23.5 7.8 %all-to-all-done.1 = f32[16,2,9,128]{3,1,2,0:T(2,128)S(1)} async-done(((f32[16,2,9,128]{3,1,2,0:T(2,128)}), f32[16,2,9,128]{3,1,2,0:T(2,128)S(1)}, u32[]{:S(2)}, u32[]{:S(2)}) %all-to-all-start.1) | async-done | bytes 147488 | tf_op jit(solution)/shard_map/all_to_all | solution.py:223
  32.2 170.7 %while.17 = (s32[]{:T(128)}, f32[16,3,256]{2,0,1:T(8,128)S(1)}, f32[16,4,9,128]{3,2,1,0:T(8,128)S(1)}, f32[16,12]{1,0:T(8,128)S(1)}, s32[16,4]{1,0:T(8,128)S(1)}...) while((s32[]{:T(128)}, f32[16,3,256]{2,0,1:T(8,128)S(1)}, ...), condition=%wide.region_13.14_spmd, body=%wide.region_1.13_spmd.sunk | while | flops 435844416 | bytes 4063208 | solution.py:247
  50.7 1.7 fusion.214
  61.4 1.7 fusion.214
  72.0 1.7 fusion.214
  82.7 1.7 fusion.214
  93.4 1.7 fusion.214
  104.0 1.7 fusion.214
  114.7 1.7 fusion.214
  125.4 1.7 fusion.214
  136.0 1.7 fusion.214
  146.7 1.7 fusion.214
  157.4 1.7 fusion.214
  168.1 1.7 fusion.214
  178.7 1.7 fusion.214
  189.4 1.7 fusion.214
  203.5 2.9 %scatter_fusion = f32[32,9,128]{2,1,0:T(8,128)S(1)} fusion(f32[32,9,128]{2,1,0:T(8,128)S(1)} %broadcast_in_dim.180, s32[64]{0:T(128)S(1)} %fusion.142, f32[64,9,128]{2,1,0:T(8,128)S(1)} %bitcast.730), kind=kCustom, calls=%fused_computation.2 | custom fusion | flops 73728 | bytes 884992 | tf_op jit(solution)/shard_map/scatter-add | solution.py:255
  206.5 10.8 %all_to_all.20 = f32[16,2,9,128]{3,1,2,0:T(2,128)S(1)} all-to-all(f32[16,2,9,128]{3,1,2,0:T(2,128)S(1)} %copy.804), channel_id=1, replica_groups=mesh['view'=2,'scene'=16] {'scene'}, dimensions={0} | all-to-all | bytes 294912 | tf_op jit(solution)/shard_map/all_to_all | solution.py:257
  217.5 1.8 scatter_fusion.1
  219.8 3.2 %all-to-all-start.3 = ((f32[2,2,9,128]{3,1,2,0:T(2,128)}), f32[2,2,9,128]{3,1,2,0:T(2,128)S(1)}, u32[]{:S(2)}, u32[]{:S(2)}) async-start(f32[2,2,9,128]{3,1,2,0:T(2,128)} %copy.807), calls=%async_computation.3 | async-start | bytes 36864 | tf_op jit(solution)/shard_map/all_to_all | solution.py:270
  223.1 30.8 %psum.7 = f32[1,12]{1,0:T(1,128)} all-reduce(f32[1,12]{1,0:T(1,128)S(1)} %bitcast.853), channel_id=1, replica_groups=mesh['view'=2,'scene'=16] {'scene'}, use_global_device_ids=true, to_apply=%region_50.51 | all-reduce | flops 12 | bytes 96 | tf_op jit(solution)/shard_map/psum | solution.py:278
  (580 shorter events, 119.0 us)
Async XLA Ops:
  0.6 0.7 copy-start.2
  1.4 0.7 copy-start
  2.4 0.7 copy-start.7
  3.1 0.7 copy-start.6
  7.0 4.4 %copy-start.5 = (s32[1,1,16,2]{2,3,1,0:T(2,128)S(1)}, s32[1,1,16,2]{2,3,1,0:T(2,128)}, u32[]{:S(2)}) copy-start(s32[1,1,16,2]{2,3,1,0:T(2,128)} %param.22) | copy-start | bytes 388
  7.0 8.2 %all-to-all-start = ((f32[2,2,9,128]{3,1,2,0:T(2,128)}), f32[2,2,9,128]{3,1,2,0:T(2,128)S(1)}, u32[]{:S(2)}, u32[]{:S(2)}) async-start(f32[2,2,9,128]{3,1,2,0:T(2,128)} %copy.793), calls=%async_computation | async-start | bytes 36864 | tf_op jit(solution)/shard_map/all_to_all | solution.py:215
  11.5 0.7 copy-start.4
  16.7 6.5 %copy-start.9 = (f32[1,12]{1,0:T(1,128)S(1)}, f32[1,12]{1,0:T(1,128)}, u32[]{:S(2)}) copy-start(f32[1,12]{1,0:T(1,128)} %param.19) | copy-start | bytes 148
  16.7 6.8 %copy-start.1 = (f32[1,16,3,256]{3,1,2,0:T(8,128)S(1)}, f32[1,16,3,256]{3,1,2,0:T(8,128)}, u32[]{:S(2)}) copy-start(f32[1,16,3,256]{3,1,2,0:T(8,128)} %param.20) | copy-start | bytes 147460
  16.7 14.7 %all-to-all-start.1 = ((f32[16,2,9,128]{3,1,2,0:T(2,128)}), f32[16,2,9,128]{3,1,2,0:T(2,128)S(1)}, u32[]{:S(2)}, u32[]{:S(2)}) async-start(f32[16,2,9,128]{3,1,2,0:T(2,128)} %fusion.49), calls=%async_computation.1 | async-start | bytes 294912 | tf_op jit(solution)/shard_map/all_to_all | solution.py:223
  31.5 0.7 copy-start.10
  202.9 0.6 copy-start.8
  219.8 34.0 %all-to-all-start.3 = ((f32[2,2,9,128]{3,1,2,0:T(2,128)}), f32[2,2,9,128]{3,1,2,0:T(2,128)S(1)}, u32[]{:S(2)}, u32[]{:S(2)}) async-start(f32[2,2,9,128]{3,1,2,0:T(2,128)} %copy.807), calls=%async_computation.3 | async-start | bytes 36864 | tf_op jit(solution)/shard_map/all_to_all | solution.py:270
  257.4 0.7 copy-start.3
where the time goes:
time: 260 us; the launch traced here: 259 us
  matrix products  91 us (35%)
  loops' own time  43.7 us (17%)
  blocking collectives  41.5 us (16%)
  local copies, waits for them, and re-layouts  31.5 us (12%)
  other arithmetic  25.2 us (10%)
  starting transfers between devices  14.1 us (5%)
  waiting for transfers between devices  10.6 us (4%)
    another operation x1, loops' own time, local(): lax.map(render_tile, (tile_ids[0], pair_slots[0], target[0]))  43.7 us
    dot_general x32, matrix products, composite(): jnp.dot(log_keep.reshape(-1, lane_count), strict, precision=lax.Precision...  41.3 us
    dot_general x48, matrix products, composite(): jnp.einsum('kpg,kcg->cp', alpha_vals * transmit, chosen_blk[:, 6:9], prec...  40.5 us
    psum x1, blocking collectives, local(): exposure_grad = lax.psum(jnp.sum(expo_terms, axis=0), 'scene')  30.8 us
    all_to_all x1, blocking collectives, local(): lax.all_to_all(grad_incoming.reshape(scene_count, capacity, feature_count...  10.8 us
    reduce_sum x16, other arithmetic, composite(): totals = jnp.sum(log_keep, axis=2)  9.52 us
    dynamic_slice x16, local copies, waits for them, and re-layouts, local(): lax.map(render_tile, (tile_ids[0], pair_slots[0], target[0]))  9.42 us
    gather x16, local copies, waits for them, and re-layouts, render_tile(): chosen = jnp.take(incoming, jnp.maximum(slot_list, 0), axis=0)  8.81 us
  transfers between devices with their start and end apart: 3, of which 2 were waited for; matrix products, arithmetic and copies ran while one was open for 0% of the time, Pallas kernels for 0%

commit v1 on v0

--- a/solution.py
+++ b/solution.py
@@ -1,6 +1,10 @@
+import functools
+
 import jax
 import jax.numpy as jnp
 from jax import lax
+from jax.experimental import pallas as pl
+from jax.experimental.pallas import tpu as pltpu
 from jax.sharding import PartitionSpec as P
 
 PIX = 256
@@ -154,38 +158,224 @@
     return jnp.concatenate([shape_rows, colour], axis=1)
 
 
-def composite(chosen_blk, live_mask, tile_id):
-    lane_count = chosen_blk.shape[2]
-    pixel_index = jnp.arange(PIX, dtype=jnp.int32)
-    pixel_x = (16 * (tile_id % TILE_COLS) + pixel_index % 16).astype(jnp.float32) + 0.5
-    pixel_y = (16 * (tile_id // TILE_COLS) + pixel_index // 16).astype(jnp.float32) + 0.5
-    gap_x = pixel_x[None, :, None] - chosen_blk[:, 0][:, None, :]
-    gap_y = pixel_y[None, :, None] - chosen_blk[:, 1][:, None, :]
-    falloff = (
-        0.5
-        * (
-            chosen_blk[:, 2][:, None, :] * gap_x * gap_x
-            + chosen_blk[:, 4][:, None, :] * gap_y * gap_y
+LOG2E = 1.4426950408889634
+FEATURES = 9
+
+
+def split_pair(values):
+    high = values.astype(jnp.bfloat16)
+    low = (values - high.astype(jnp.float32)).astype(jnp.bfloat16)
+    return jnp.concatenate([high, low], axis=1)
+
+
+def render_kernel(
+    tile_ids,
+    slots,
+    exposure,
+    incoming,
+    target,
+    shown,
+    grads,
+    weight,
+    ratio,
+    weight_pair,
+    expo_sum,
+    before_mat,
+    after_mat,
+    powers,
+):
+    tile_count, slot_count = slots.shape
+    lanes = incoming.shape[2]
+    row_at = lax.broadcasted_iota(jnp.int32, (2 * lanes, 2 * lanes), 0) % lanes
+    col_at = lax.broadcasted_iota(jnp.int32, (2 * lanes, 2 * lanes), 1)
+    total = col_at >= lanes
+    before_mat[...] = jnp.where(total | (row_at < col_at), 1.0, 0.0).astype(jnp.bfloat16)
+    after_mat[...] = jnp.where(total | (row_at > col_at), 1.0, 0.0).astype(jnp.bfloat16)
+    power_at = lax.broadcasted_iota(jnp.int32, (8, PIX), 0)
+    pixel_at = lax.broadcasted_iota(jnp.int32, (8, PIX), 1)
+    side_x = (pixel_at % 16).astype(jnp.float32) - 7.5
+    side_y = (pixel_at // 16).astype(jnp.float32) - 7.5
+    picks = [jnp.ones_like(side_x), side_x, side_y, side_x * side_x, side_x * side_y, side_y * side_y]
+    table = jnp.zeros((8, PIX), jnp.float32)
+    for at, pick in enumerate(picks):
+        table = jnp.where(power_at == at, pick, table)
+    powers[...] = table.astype(jnp.bfloat16)
+    grads[...] = jnp.zeros_like(grads)
+    expo_sum[...] = jnp.zeros_like(expo_sum)
+    mixing = [
+        [exposure[0, 3 * i + j] + (1.0 if i == j else 0.0) for j in range(3)] for i in range(3)
+    ]
+    offset = [exposure[0, 9 + i] for i in range(3)]
+    local_x = [
+        lax.broadcasted_iota(jnp.int32, (8, lanes), 0).astype(jnp.float32) + (8.0 * half - 7.5)
+        for half in range(2)
+    ]
+    zero_rows = jnp.zeros((2, lanes), jnp.float32)
+
+    def load(tile, at, centre_x, centre_y):
+        block = incoming[slots[tile, at]]
+        rows = [block[i : i + 1] for i in range(FEATURES)]
+        rows[0] = rows[0] - centre_x
+        rows[1] = rows[1] - centre_y
+        return rows, block[6:9]
+
+    def one_tile(tile, live):
+        tile_id = tile_ids[0, tile]
+        centre_x = (16 * (tile_id % TILE_COLS) + 8).astype(jnp.float32)
+        centre_y = (16 * (tile_id // TILE_COLS) + 8).astype(jnp.float32)
+        carry = None
+        shade = None
+        for at in range(live):
+            rows, colour = load(tile, at, centre_x, centre_y)
+            wide = [jnp.broadcast_to(row, (8, lanes)) for row in rows[:6]]
+            gap_x = [side - wide[0] for side in local_x]
+            scaled_a = wide[2] * (-0.5 * LOG2E)
+            scaled_b = wide[3] * (-LOG2E)
+            scaled_c = wide[4] * (-0.5 * LOG2E)
+            part_x = [scaled_a * gap * gap for gap in gap_x]
+            pieces = []
+            for line in range(PIX // 16):
+                gap_y = (line - 7.5) - wide[1]
+                part_y = scaled_c * gap_y * gap_y
+                slope = scaled_b * gap_y
+                for half in range(2):
+                    pieces.append(
+                        wide[5] * jnp.exp2(part_x[half] + gap_x[half] * slope + part_y)
+                    )
+            alpha = jnp.concatenate(pieces, axis=0)
+            log_keep = jnp.log(1.0 - alpha)
+            sums = jnp.dot(
+                split_pair(log_keep), before_mat[...], preferred_element_type=jnp.float32
+            )
+            inside = sums[:, :lanes]
+            if at > 0:
+                inside = inside + carry
+            if at + 1 < live:
+                carry = sums[:, lanes:] if at == 0 else carry + sums[:, lanes:]
+            seen = alpha * jnp.exp(inside)
+            pair = split_pair(seen)
+            weight[at] = seen
+            ratio[at] = alpha * jnp.exp(-log_keep)
+            weight_pair[at] = pair
+            high = colour.astype(jnp.bfloat16).astype(jnp.float32)
+            low = colour - high
+            left = jnp.concatenate([high, low, zero_rows], axis=0)
+            right = jnp.concatenate([high, jnp.zeros((5, lanes), jnp.float32)], axis=0)
+            mixed = jnp.concatenate([left, right], axis=1).astype(jnp.bfloat16)
+            term = lax.dot_general(
+                mixed, pair, (((1,), (1,)), ((), ())), preferred_element_type=jnp.float32
+            )
+            shade = term if at == 0 else shade + term
+        goal = target[0, tile]
+        tone = [shade[i : i + 1] + shade[i + 3 : i + 4] for i in range(3)]
+        image = [
+            mixing[i][0] * tone[0] + mixing[i][1] * tone[1] + mixing[i][2] * tone[2] + offset[i]
+            for i in range(3)
+        ]
+        shown[0, tile] = jnp.concatenate(image, axis=0)
+        miss = [image[i] - goal[i : i + 1] for i in range(3)]
+        expo_sum[...] += jnp.concatenate(
+            [miss[i] * tone[j] for i in range(3) for j in range(3)] + miss, axis=0
         )
-        + chosen_blk[:, 3][:, None, :] * gap_x * gap_y
-    )
-    alpha_vals = (
-        chosen_blk[:, 5][:, None, :]
-        * jnp.exp(-falloff)
-        * live_mask.astype(jnp.float32)[:, None, None]
-    )
-    log_keep = jnp.log1p(-alpha_vals)
-    lane_index = jnp.arange(lane_count)
-    strict = (lane_index[:, None] < lane_index[None, :]).astype(jnp.float32)
-    inside = jnp.dot(
-        log_keep.reshape(-1, lane_count), strict, precision=lax.Precision.HIGHEST
-    ).reshape(log_keep.shape)
-    totals = jnp.sum(log_keep, axis=2)
-    before = jnp.cumsum(totals, axis=0) - totals
-    transmit = jnp.exp(inside + before[:, :, None])
-    return jnp.einsum(
-        "kpg,kcg->cp", alpha_vals * transmit, chosen_blk[:, 6:9], precision=lax.Precision.HIGHEST
-    )
+        back = jnp.concatenate(
+            [
+                mixing[0][j] * miss[0] + mixing[1][j] * miss[1] + mixing[2][j] * miss[2]
+                for j in range(3)
+            ],
+            axis=0,
+        )
+        back_high = back.astype(jnp.bfloat16).astype(jnp.float32)
+        back_low = back - back_high
+        back_left = jnp.concatenate(
+            [back_high, back_low, jnp.zeros((2, PIX), jnp.float32)], axis=0
+        ).astype(jnp.bfloat16)
+        back_side = jnp.transpose(
+            jnp.concatenate(
+                [back_high, back_high, back_low, jnp.zeros((7, PIX), jnp.float32)], axis=0
+            )
+        ).astype(jnp.bfloat16)
+        carry = None
+        for at in reversed(range(live)):
+            rows, colour = load(tile, at, centre_x, centre_y)
+            high = colour.astype(jnp.bfloat16).astype(jnp.float32)
+            low = colour - high
+            colour_side = jnp.concatenate(
+                [high, low, high, jnp.zeros((7, lanes), jnp.float32)], axis=0
+            ).astype(jnp.bfloat16)
+            pull = jnp.dot(back_side, colour_side, preferred_element_type=jnp.float32)
+            gain = weight[at] * pull
+            sums = jnp.dot(split_pair(gain), after_mat[...], preferred_element_type=jnp.float32)
+            behind = sums[:, :lanes]
+            if at + 1 < live:
+                behind = behind + carry
+            if at > 0:
+                carry = sums[:, lanes:] if at + 1 == live else carry + sums[:, lanes:]
+            heat = gain - behind * ratio[at]
+            moments = jnp.dot(powers[...], split_pair(heat), preferred_element_type=jnp.float32)
+            moments = moments[:, :lanes] + moments[:, lanes:]
+            tint = jnp.dot(back_left, weight_pair[at], preferred_element_type=jnp.float32)
+            tint = tint[:, :lanes] + tint[:, lanes:]
+            tint = tint[0:3] + tint[3:6]
+            pos_x, pos_y, con_a, con_b, con_c, opacity = rows[:6]
+            m_one, m_x, m_y, m_xx, m_xy, m_yy = [moments[i : i + 1] for i in range(6)]
+            d_x = m_x - pos_x * m_one
+            d_y = m_y - pos_y * m_one
+            d_xx = m_xx - pos_x * (m_x + d_x)
+            d_xy = m_xy - pos_x * m_y - pos_y * d_x
+            d_yy = m_yy - pos_y * (m_y + d_y)
+            grads[slots[tile, at], 0:FEATURES] += jnp.concatenate(
+                [
+                    con_a * d_x + con_b * d_y,
+                    con_b * d_x + con_c * d_y,
+                    -0.5 * d_xx,
+                    -d_xy,
+                    -0.5 * d_yy,
+                    m_one / opacity,
+                    tint,
+                ],
+                axis=0,
+            )
+
+    def tile_step(tile, unused):
+        live = jnp.int32(0)
+        for at in range(slot_count):
+            live = live + jnp.where(slots[tile, at] >= 0, 1, 0)
+        for number in range(1, slot_count + 1):
+            pl.when(live == number)(functools.partial(one_tile, tile, number))
+        return unused
+
+    lax.fori_loop(0, tile_count, tile_step, 0)
+    sums = jnp.sum(expo_sum[...], axis=1, keepdims=True)
+    lane_at = lax.broadcasted_iota(jnp.int32, (12, lanes), 1)
+    row_at = lax.broadcasted_iota(jnp.int32, (12, lanes), 0)
+    spread = jnp.sum(jnp.where(lane_at == row_at, sums, 0.0), axis=0, keepdims=True)
+    grads[:, FEATURES : FEATURES + 1] = jnp.broadcast_to(spread[None], (grads.shape[0], 1, lanes))
+
+
+def render(tile_ids, slots, exposure, incoming, target):
+    slot_count = slots.shape[1]
+    lanes = incoming.shape[2]
+    smem = pl.BlockSpec(memory_space=pltpu.SMEM)
+    vmem = pl.BlockSpec(memory_space=pltpu.VMEM)
+    return pl.pallas_call(
+        render_kernel,
+        out_shape=(
+            jax.ShapeDtypeStruct(target.shape, jnp.float32),
+            jax.ShapeDtypeStruct((incoming.shape[0], FEATURES + 1, lanes), jnp.float32),
+        ),
+        in_specs=[smem, smem, smem, vmem, vmem],
+        out_specs=(vmem, vmem),
+        scratch_shapes=[
+            pltpu.VMEM((slot_count, PIX, lanes), jnp.float32),
+            pltpu.VMEM((slot_count, PIX, lanes), jnp.float32),
+            pltpu.VMEM((slot_count, PIX, 2 * lanes), jnp.bfloat16),
+            pltpu.VMEM((12, PIX), jnp.float32),
+            pltpu.VMEM((2 * lanes, 2 * lanes), jnp.bfloat16),
+            pltpu.VMEM((2 * lanes, 2 * lanes), jnp.bfloat16),
+            pltpu.VMEM((8, PIX), jnp.bfloat16),
+        ],
+        compiler_params=pltpu.CompilerParams(vmem_limit_bytes=32 * 1024 * 1024),
+    )(tile_ids, slots, exposure, incoming, target)
 
 
 def local(
@@ -223,44 +413,16 @@
     incoming = lax.all_to_all(outgoing, "scene", split_axis=0, concat_axis=0, tiled=True).reshape(
         scene_count * capacity, feature_count, lane_count
     )
-    mixing = jnp.eye(3, dtype=jnp.float32) + exposure[0, 0:9].reshape(3, 3)
-    offset = exposure[0, 9:12]
-
-    def render_tile(tile_items):
-        tile_id, slot_list, goal_tile = tile_items
-        live_mask = slot_list >= 0
-        chosen = jnp.take(incoming, jnp.maximum(slot_list, 0), axis=0)
-        colour, shade_back = jax.vjp(
-            lambda chosen_blk: composite(chosen_blk, live_mask, tile_id), chosen
-        )
-        shown_tile = jnp.dot(mixing, colour, precision=lax.Precision.HIGHEST) + offset[:, None]
-        miss_tile = shown_tile - goal_tile
-        grad_chosen = shade_back(jnp.dot(mixing.T, miss_tile, precision=lax.Precision.HIGHEST))[0]
-        expo_terms = jnp.concatenate(
-            [
-                jnp.dot(miss_tile, colour.T, precision=lax.Precision.HIGHEST).reshape(9),
-                jnp.sum(miss_tile, axis=1),
-            ]
-        )
-        return (shown_tile, grad_chosen, expo_terms)
-
-    shown_tiles, grad_chosen, expo_terms = lax.map(
-        render_tile, (tile_ids[0], pair_slots[0], target[0])
-    )
-    dump_index = scene_count * capacity
-    where_to = jnp.where(pair_slots[0] >= 0, pair_slots[0], dump_index).reshape(-1)
-    grad_incoming = (
-        jnp.zeros((dump_index, feature_count, lane_count), jnp.float32)
-        .at[where_to]
-        .add(grad_chosen.reshape(-1, feature_count, lane_count), mode="drop")
-    )
+    shown_tiles, grad_incoming = render(tile_ids, pair_slots[0], exposure, incoming, target)
     returned = lax.all_to_all(
-        grad_incoming.reshape(scene_count, capacity, feature_count, lane_count),
+        grad_incoming.reshape(scene_count, capacity, feature_count + 1, lane_count),
         "scene",
         split_axis=0,
         concat_axis=0,
         tiled=True,
     )
+    exposure_grad = jnp.sum(returned[:, 0, feature_count, 0:12], axis=0)
+    returned = returned[:, :, 0:feature_count]
     home_index = jnp.where(send_picks >= 0, send_picks, owned_count).reshape(-1)
     grad_projected = (
         jnp.zeros((owned_count, feature_count, lane_count), jnp.float32)
@@ -275,9 +437,8 @@
         tiled=True,
     )
     param_grads = unproject(sent_back)
-    exposure_grad = lax.psum(jnp.sum(expo_terms, axis=0), "scene")
     return (
-        shown_tiles[None],
+        shown_tiles,
         param_grads[0],
         param_grads[1],
         param_grads[2],

time: 260 us -> 88.1 us (0.34)
  matrix products: 91 us -> 0 us
  loops' own time: 43.7 us -> 0 us
  blocking collectives: 41.5 us -> 0 us
  Pallas kernels: 0 us -> 27.4 us
  local copies, waits for them, and re-layouts: 31.5 us -> 10.9 us
  other arithmetic: 25.2 us -> 8 us
  waiting for transfers between devices: 10.6 us -> 22 us
  starting transfers between devices: 14.1 us -> 18.2 us
    dot_general x128 -> x0, matrix products: 91 us -> none  [the longest x32 41.3 us: composite(): jnp.dot(log_keep.reshape(-1, lane_count), strict, precision=lax.Precision...]
    another operation x1 -> x0, loops' own time: 43.7 us -> none  [local(): lax.map(render_tile, (tile_ids[0], pair_slots[0], target[0]))]
    psum x1 -> x0, blocking collectives: 30.8 us -> none  [local(): exposure_grad = lax.psum(jnp.sum(expo_terms, axis=0), 'scene')]
    pallas_call x0 -> x1, Pallas kernels: none -> 27.4 us  [render(): pl.pallas_call(render_kernel, out_shape=(jax.ShapeDtypeStruct(target.shap...]
    all_to_all x1 -> x0, blocking collectives: 10.8 us -> none  [local(): lax.all_to_all(grad_incoming.reshape(scene_count, capacity, feature_count...]
    dynamic_slice x16 -> x0, local copies, waits for them, and re-layouts: 9.42 us -> none  [local(): lax.map(render_tile, (tile_ids[0], pair_slots[0], target[0]))]
    reduce_sum x17 -> x1, other arithmetic: 9.55 us -> 0.54 us  [local(): exposure_grad = jnp.sum(returned[:, 0, feature_count, 0:12], axis=0)]
    gather x16 -> x0, local copies, waits for them, and re-layouts: 8.81 us -> none  [render_tile(): chosen = jnp.take(incoming, jnp.maximum(slot_list, 0), axis=0)]
  transfers between devices with their start and end apart: 3 -> 4, of which waited for: 2 -> 4; matrix products, arithmetic and copies ran while one was open for 0% -> 2% of each run, Pallas kernels for 0% -> 0%
where the time goes in v1:
time: 88.1 us; the launch traced here: 87.5 us
  Pallas kernels  27.4 us (31%)
  waiting for transfers between devices  22 us (25%)
  starting transfers between devices  18.2 us (21%)
  local copies, waits for them, and re-layouts  10.9 us (12%)
  other arithmetic  8 us (9%)
  between operations  1.11 us (1%)
    pallas_call x1, Pallas kernels, render(): pl.pallas_call(render_kernel, out_shape=(jax.ShapeDtypeStruct(target.shap...  27.4 us
    all_to_all x1, waiting for transfers between devices, local(): lax.all_to_all(grad_incoming.reshape(scene_count, capacity, feature_count...  7.79 us
    all_to_all x1, waiting for transfers between devices, local(): lax.all_to_all(outgoing, 'scene', split_axis=0, concat_axis=0, tiled=True)  7.42 us
    unnamed x28, local copies, waits for them, and re-layouts  6.51 us
    all_to_all x1, starting transfers between devices, local(): lax.all_to_all(outgoing, 'scene', split_axis=0, concat_axis=0, tiled=True)  6.48 us
    all_to_all x1, starting transfers between devices, local(): lax.all_to_all(own_proj, 'view', split_axis=0, concat_axis=0, tiled=True)  4.37 us
    all_to_all x1, starting transfers between devices, local(): lax.all_to_all(grad_projected.reshape(view_count, per_device, feature_cou...  3.79 us
    all_to_all x1, starting transfers between devices, local(): lax.all_to_all(grad_incoming.reshape(scene_count, capacity, feature_count...  3.52 us
  transfers between devices with their start and end apart: 4, of which 4 were waited for; matrix products, arithmetic and copies ran while one was open for 2% of the time, Pallas kernels for 0%

profile of v1, /device:TPU:0, one launch (start us, length us, event | category | flops | bytes accessed | tf_op | source)
XLA Modules:
  0.0 87.5 jit_solution(5669203532662326755)
XLA Ops:
  0.6 0.7 slice.154
  1.3 0.7 copy-done.5
  2.1 0.7 copy-done.6
  2.7 0.7 copy-done.2
  6.4 0.7 copy-done.8
  7.5 0.6 copy.787
  8.1 4.4 %all-to-all-start = ((f32[2,2,9,128]{3,1,2,0:T(2,128)}), f32[2,2,9,128]{3,1,2,0:T(2,128)S(1)}, u32[]{:S(2)}, u32[]{:S(2)}) async-start(f32[2,2,9,128]{3,1,2,0:T(2,128)} %copy.787), calls=%async_computation | async-start | bytes 36864 | tf_op jit(solution)/shard_map/all_to_all | solution.py:405
  12.8 3.5 %all-to-all-done = f32[2,2,9,128]{3,1,2,0:T(2,128)S(1)} async-done(((f32[2,2,9,128]{3,1,2,0:T(2,128)}), f32[2,2,9,128]{3,1,2,0:T(2,128)S(1)}, u32[]{:S(2)}, u32[]{:S(2)}) %all-to-all-start) | async-done | bytes 18464 | tf_op jit(solution)/shard_map/all_to_all | solution.py:405
  16.9 0.8 fusion
  17.7 6.5 %all-to-all-start.1 = ((f32[16,2,9,128]{3,1,2,0:T(2,128)}), f32[16,2,9,128]{3,1,2,0:T(2,128)S(1)}, u32[]{:S(2)}, u32[]{:S(2)}) async-start(f32[16,2,9,128]{3,1,2,0:T(2,128)} %fusion), calls=%async_computation.1 | async-start | bytes 294912 | tf_op jit(solution)/shard_map/all_to_all | solution.py:413
  24.3 0.6 copy-done.10
  25.0 7.4 %all-to-all-done.1 = f32[16,2,9,128]{3,1,2,0:T(2,128)S(1)} async-done(((f32[16,2,9,128]{3,1,2,0:T(2,128)}), f32[16,2,9,128]{3,1,2,0:T(2,128)S(1)}, u32[]{:S(2)}, u32[]{:S(2)}) %all-to-all-start.1) | async-done | bytes 147488 | tf_op jit(solution)/shard_map/all_to_all | solution.py:413
  32.5 0.6 copy-done
  33.1 27.4 %shard_map.162 = (f32[1,16,3,256]{3,2,1,0:T(4,128)S(1)}, f32[32,10,128]{2,1,0:T(8,128)S(1)}) custom-call(s32[1,16]{1,0:T(1,128)S(1)} %copy-done, s32[16,4]{1,0:T(8,128)S(1)} %copy.793.slots, f32[1,12]{1,0:T(1,128)S(1)} %copy-done.1, f32[32,9,128]{2,1,0:T(8,128)S(1)} %bitcast.542, f32[1,16,3,256]{3,2,1,0:T(4,128)S(1)} %copy.794.target), custom_call_target="tpu_custom_call" | custom-call | tf_op jit(solution)/shard_map/pallas_call | solution.py:360
  60.5 0.7 copy.795
  61.2 3.5 %all-to-all-start.2 = ((f32[16,2,10,128]{3,1,2,0:T(2,128)}), f32[16,2,10,128]{3,1,2,0:T(2,128)S(1)}, u32[]{:S(2)}, u32[]{:S(2)}) async-start(f32[16,2,10,128]{3,1,2,0:T(2,128)} %copy.795), calls=%async_computation.2 | async-start | bytes 327680 | tf_op jit(solution)/shard_map/all_to_all | solution.py:417
  64.8 0.6 copy.888
  65.4 7.8 %all-to-all-done.2 = f32[16,2,10,128]{3,1,2,0:T(2,128)S(1)} async-done(((f32[16,2,10,128]{3,1,2,0:T(2,128)}), f32[16,2,10,128]{3,1,2,0:T(2,128)S(1)}, u32[]{:S(2)}, u32[]{:S(2)}) %all-to-all-start.2) | async-done | bytes 163872 | tf_op jit(solution)/shard_map/all_to_all | solution.py:417
  73.4 1.8 %scatter_fusion = f32[4,9,128]{2,1,0:T(8,128)S(1)} fusion(f32[4,9,128]{2,1,0:T(8,128)S(1)} %broadcast_in_dim.26, s32[32]{0:T(128)S(1)} %get-tuple-element.273, f32[32,9,128]{2,1,0:T(8,128)S(1)} %copy.797), kind=kCustom, calls=%fused_computation.1 | custom fusion | flops 36864 | bytes 442496 | tf_op jit(solution)/shard_map/scatter-add | solution.py:430
  75.1 0.6 copy.798
  75.8 3.8 %all-to-all-start.3 = ((f32[2,2,9,128]{3,1,2,0:T(2,128)}), f32[2,2,9,128]{3,1,2,0:T(2,128)S(1)}, u32[]{:S(2)}, u32[]{:S(2)}) async-start(f32[2,2,9,128]{3,1,2,0:T(2,128)} %copy.798), calls=%async_computation.3 | async-start | bytes 36864 | tf_op jit(solution)/shard_map/all_to_all | solution.py:432
  80.1 3.3 %all-to-all-done.3 = f32[2,2,9,128]{3,1,2,0:T(2,128)S(1)} async-done(((f32[2,2,9,128]{3,1,2,0:T(2,128)}), f32[2,2,9,128]{3,1,2,0:T(2,128)S(1)}, u32[]{:S(2)}, u32[]{:S(2)}) %all-to-all-start.3) | async-done | bytes 18464 | tf_op jit(solution)/shard_map/all_to_all | solution.py:432
  84.0 0.6 copy.889
  86.4 0.6 pad_add_fusion
  (105 shorter events, 7.9 us)
Async XLA Ops:
  1.3 0.7 copy-start.5
  2.0 0.7 copy-start.6
  2.7 0.7 copy-start.2
  3.7 0.7 copy-start.9
  5.5 0.8 copy-start.4
  6.4 0.7 copy-start.8
  8.1 4.4 %copy-start.7 = (s32[1,1,16,2]{2,3,1,0:T(2,128)S(1)}, s32[1,1,16,2]{2,3,1,0:T(2,128)}, u32[]{:S(2)}) copy-start(s32[1,1,16,2]{2,3,1,0:T(2,128)} %param.20) | copy-start | bytes 388
  8.1 8.2 %all-to-all-start = ((f32[2,2,9,128]{3,1,2,0:T(2,128)}), f32[2,2,9,128]{3,1,2,0:T(2,128)S(1)}, u32[]{:S(2)}, u32[]{:S(2)}) async-start(f32[2,2,9,128]{3,1,2,0:T(2,128)} %copy.787), calls=%async_computation | async-start | bytes 36864 | tf_op jit(solution)/shard_map/all_to_all | solution.py:405
  17.7 6.5 %copy-start.3 = (f32[1,16,3,256]{3,1,2,0:T(8,128)S(1)}, f32[1,16,3,256]{3,1,2,0:T(8,128)}, u32[]{:S(2)}) copy-start(f32[1,16,3,256]{3,1,2,0:T(8,128)} %param.18) | copy-start | bytes 147460
  17.7 14.7 %all-to-all-start.1 = ((f32[16,2,9,128]{3,1,2,0:T(2,128)}), f32[16,2,9,128]{3,1,2,0:T(2,128)S(1)}, u32[]{:S(2)}, u32[]{:S(2)}) async-start(f32[16,2,9,128]{3,1,2,0:T(2,128)} %fusion), calls=%async_computation.1 | async-start | bytes 294912 | tf_op jit(solution)/shard_map/all_to_all | solution.py:413
  24.2 0.7 copy-start.10
  32.5 0.7 copy-start
  32.5 0.7 copy-start.1
  61.2 11.9 %all-to-all-start.2 = ((f32[16,2,10,128]{3,1,2,0:T(2,128)}), f32[16,2,10,128]{3,1,2,0:T(2,128)S(1)}, u32[]{:S(2)}, u32[]{:S(2)}) async-start(f32[16,2,10,128]{3,1,2,0:T(2,128)} %copy.795), calls=%async_computation.2 | async-start | bytes 327680 | tf_op jit(solution)/shard_map/all_to_all | solution.py:417
  75.8 7.7 %all-to-all-start.3 = ((f32[2,2,9,128]{3,1,2,0:T(2,128)}), f32[2,2,9,128]{3,1,2,0:T(2,128)S(1)}, u32[]{:S(2)}, u32[]{:S(2)}) async-start(f32[2,2,9,128]{3,1,2,0:T(2,128)} %copy.798), calls=%async_computation.3 | async-start | bytes 36864 | tf_op jit(solution)/shard_map/all_to_all | solution.py:432

commit v2 on v1

--- a/solution.py
+++ b/solution.py
@@ -10,6 +10,7 @@
 PIX = 256
 TILE_COLS = 32
 
+FEATURES = 9
 
 SH_ZERO = 0.28209479177387814
 SH_ONE = 0.4886025119029199
@@ -51,25 +52,23 @@
         SH_THREE[5] * dir_z * (sq_x - sq_y),
         SH_THREE[6] * dir_x * (sq_x - 3.0 * sq_y),
     ]
-    return jnp.stack(sh_basis, axis=1)
-
-
-def project(pieces, camera):
-    means, log_scales, rotations, opacity_logits, colour_coefs = pieces
-    rotation = camera[0:9].reshape(3, 3)
+    return sh_basis
+
+
+def project(camera, position, log_scales, rotations, opacity_logits, colour_coefs):
+    rotation = [camera[0:3], camera[3:6], camera[6:9]]
     translation = camera[9:12]
-    focal_x, focal_y, centre_x, centre_y = (camera[12], camera[13], camera[14], camera[15])
-    position = [means[:, 0], means[:, 1], means[:, 2]]
+    focal_x, focal_y, centre_x, centre_y = camera[12:16]
     view_pos = [
-        rotation[row_at, 0] * position[0]
-        + rotation[row_at, 1] * position[1]
-        + rotation[row_at, 2] * position[2]
+        rotation[row_at][0] * position[0]
+        + rotation[row_at][1] * position[1]
+        + rotation[row_at][2] * position[2]
         + translation[row_at]
         for row_at in range(3)
     ]
     inv_depth = 1.0 / view_pos[2]
-    quat_w = rotations[:, 0] + 3.0
-    quat_x, quat_y, quat_z = (rotations[:, 1], rotations[:, 2], rotations[:, 3])
+    quat_w = rotations[0] + 3.0
+    quat_x, quat_y, quat_z = (rotations[1], rotations[2], rotations[3])
     quat_norm = jnp.sqrt(quat_w * quat_w + quat_x * quat_x + quat_y * quat_y + quat_z * quat_z)
     quat_w, quat_x, quat_y, quat_z = (
         quat_w / quat_norm,
@@ -94,20 +93,20 @@
             1.0 - 2.0 * (quat_x * quat_x + quat_y * quat_y),
         ],
     ]
-    scales = jnp.exp(log_scales)
+    scales = [jnp.exp(row) for row in log_scales]
     world_frame = [
-        [spin_matrix[row_at][col_at] * scales[:, col_at] for col_at in range(3)]
+        [spin_matrix[row_at][col_at] * scales[col_at] for col_at in range(3)]
         for row_at in range(3)
     ]
     jacobian = [
         [
-            focal_x * inv_depth * rotation[0, col_at]
-            - focal_x * view_pos[0] * inv_depth * inv_depth * rotation[2, col_at]
+            focal_x * inv_depth * rotation[0][col_at]
+            - focal_x * view_pos[0] * inv_depth * inv_depth * rotation[2][col_at]
             for col_at in range(3)
         ],
         [
-            focal_y * inv_depth * rotation[1, col_at]
-            - focal_y * view_pos[1] * inv_depth * inv_depth * rotation[2, col_at]
+            focal_y * inv_depth * rotation[1][col_at]
+            - focal_y * view_pos[1] * inv_depth * inv_depth * rotation[2][col_at]
             for col_at in range(3)
         ],
     ]
@@ -130,36 +129,35 @@
     determinant = sigma_xx * sigma_yy - sigma_xy * sigma_xy
     screen_x = focal_x * view_pos[0] * inv_depth + centre_x
     screen_y = focal_y * view_pos[1] * inv_depth + centre_y
-    opacity = jax.nn.sigmoid(opacity_logits[:, 0])
+    opacity = jax.nn.sigmoid(opacity_logits)
     eye_pos = [
         -(
-            rotation[0, col_at] * translation[0]
-            + rotation[1, col_at] * translation[1]
-            + rotation[2, col_at] * translation[2]
+            rotation[0][col_at] * translation[0]
+            + rotation[1][col_at] * translation[1]
+            + rotation[2][col_at] * translation[2]
         )
         for col_at in range(3)
     ]
     offsets = [position[col_at] - eye_pos[col_at] for col_at in range(3)]
     eye_dist = jnp.sqrt(offsets[0] ** 2 + offsets[1] ** 2 + offsets[2] ** 2)
     sh_basis = harmonics(offsets[0] / eye_dist, offsets[1] / eye_dist, offsets[2] / eye_dist)
-    sh_coefs = colour_coefs.reshape(colour_coefs.shape[0], 16, 3, colour_coefs.shape[2])
-    colour = jnp.maximum(0.5 + jnp.sum(sh_basis[:, :, None, :] * sh_coefs, axis=1), 0.0)
-    shape_rows = jnp.stack(
-        [
-            screen_x,
-            screen_y,
-            sigma_yy / determinant,
-            -sigma_xy / determinant,
-            sigma_xx / determinant,
-            opacity,
-        ],
-        axis=1,
-    )
-    return jnp.concatenate([shape_rows, colour], axis=1)
+    colour = []
+    for channel in range(3):
+        total = sh_basis[0] * colour_coefs[channel]
+        for order in range(1, 16):
+            total = total + sh_basis[order] * colour_coefs[3 * order + channel]
+        colour.append(jnp.maximum(0.5 + total, 0.0))
+    return [
+        screen_x,
+        screen_y,
+        sigma_yy / determinant,
+        -sigma_xy / determinant,
+        sigma_xx / determinant,
+        opacity,
+    ] + colour
 
 
 LOG2E = 1.4426950408889634
-FEATURES = 9
 
 
 def split_pair(values):
@@ -375,7 +373,297 @@
             pltpu.VMEM((8, PIX), jnp.bfloat16),
         ],
         compiler_params=pltpu.CompilerParams(vmem_limit_bytes=32 * 1024 * 1024),
+        name="render",
     )(tile_ids, slots, exposure, incoming, target)
+
+
+def padded(rows):
+    return (rows + 7) // 8 * 8
+
+
+def camera_rows(cameras, block_count):
+    view_count = cameras.shape[0]
+    shape = (view_count * block_count, 128)
+    view_at = lax.broadcasted_iota(jnp.int32, shape, 0) // block_count
+    entries = []
+    for entry in range(16):
+        value = jnp.full(shape, cameras[0, entry])
+        for view in range(1, view_count):
+            value = jnp.where(view_at == view, cameras[view, entry], value)
+        entries.append(value)
+    return entries
+
+
+def parameter_rows(refs, view_count):
+    block_count = refs[0].shape[0]
+
+    def row(ref, at):
+        own = [ref[block, at : at + 1] for block in range(block_count)]
+        return jnp.concatenate(own * view_count, axis=0)
+
+    means, log_scales, rotations, opacity_logits, colour_coefs = refs
+    return (
+        [row(means, at) for at in range(3)],
+        [row(log_scales, at) for at in range(3)],
+        [row(rotations, at) for at in range(4)],
+        row(opacity_logits, 0),
+        [row(colour_coefs, at) for at in range(48)],
+    )
+
+
+def fill(rows, count, lanes):
+    return rows if count == 0 else rows + [jnp.zeros((count, lanes), jnp.float32)]
+
+
+def greet(view_count, scene_count, view, scene):
+    barrier = pltpu.get_barrier_semaphore()
+    for step in range(1, view_count):
+        pl.semaphore_signal(
+            barrier,
+            inc=1,
+            device_id=(lax.rem(view + step, view_count), scene),
+            device_id_type=pl.DeviceIdType.MESH,
+        )
+
+    def to_scene(step, unused):
+        pl.semaphore_signal(
+            barrier,
+            inc=1,
+            device_id=(view, lax.rem(scene + step, scene_count)),
+            device_id_type=pl.DeviceIdType.MESH,
+        )
+        return unused
+
+    lax.fori_loop(1, scene_count, to_scene, 0)
+    return barrier
+
+
+def view_copy(outbox, inbox, sems, step, view, scene, view_count):
+    peer = lax.rem(view + step, view_count)
+    return pltpu.make_async_remote_copy(
+        src_ref=outbox.at[peer],
+        dst_ref=inbox.at[view],
+        send_sem=sems[0].at[step],
+        recv_sem=sems[1].at[step],
+        device_id=(peer, scene),
+        device_id_type=pl.DeviceIdType.MESH,
+    )
+
+
+def scene_copy(outbox, inbox, sems, step, view, scene, scene_count):
+    peer = lax.rem(scene + step, scene_count)
+    return pltpu.make_async_remote_copy(
+        src_ref=outbox.at[peer],
+        dst_ref=inbox.at[scene],
+        send_sem=sems[0].at[step],
+        recv_sem=sems[1].at[step],
+        device_id=(view, peer),
+        device_id_type=pl.DeviceIdType.MESH,
+    )
+
+
+def spread_kernel(
+    view_count,
+    scene_count,
+    cameras,
+    send,
+    means,
+    log_scales,
+    rotations,
+    opacity_logits,
+    colour_coefs,
+    incoming,
+    view_out,
+    view_in,
+    blocks,
+    scene_out,
+    scene_in,
+    view_send,
+    view_recv,
+    scene_send,
+    scene_recv,
+):
+    view, scene = lax.axis_index("view"), lax.axis_index("scene")
+    capacity = send.shape[1]
+    block_count, lanes = means.shape[0], means.shape[2]
+    barrier = greet(view_count, scene_count, view, scene)
+    rows = project(
+        camera_rows(cameras, block_count),
+        *parameter_rows((means, log_scales, rotations, opacity_logits, colour_coefs), view_count),
+    )
+    for target in range(view_count):
+        parts = []
+        for block in range(block_count):
+            at = target * block_count + block
+            parts += [row[at : at + 1] for row in rows]
+        spare = view_out.shape[1] - block_count * FEATURES
+        view_out[target] = jnp.concatenate(fill(parts, spare, lanes), axis=0)
+    pl.semaphore_wait(barrier, view_count + scene_count - 2)
+    view_sems = (view_send, view_recv)
+    for step in range(1, view_count):
+        view_copy(view_out, view_in, view_sems, step, view, scene, view_count).start()
+    view_in[view] = view_out[view]
+    for step in range(1, view_count):
+        view_copy(view_out, view_in, view_sems, step, view, scene, view_count).wait()
+    for source in range(view_count):
+        for block in range(block_count):
+            blocks[source * block_count + block] = view_in[
+                source, block * FEATURES : (block + 1) * FEATURES
+            ]
+    spare = scene_out.shape[1] - capacity * FEATURES
+
+    def choose(peer, unused):
+        parts = [blocks[jnp.maximum(send[peer, at], 0)] for at in range(capacity)]
+        scene_out[peer] = jnp.concatenate(fill(parts, spare, lanes), axis=0)
+        return unused
+
+    def start(step, unused):
+        choose(lax.rem(scene + step, scene_count), 0)
+        scene_copy(scene_out, scene_in, scene_sems, step, view, scene, scene_count).start()
+        return unused
+
+    def place(source, box):
+        for at in range(capacity):
+            incoming[source * capacity + at] = box[at * FEATURES : (at + 1) * FEATURES]
+
+    def finish(step, unused):
+        scene_copy(scene_out, scene_in, scene_sems, step, view, scene, scene_count).wait()
+        source = lax.rem(scene - step + scene_count, scene_count)
+        place(source, scene_in[source])
+        return unused
+
+    scene_sems = (scene_send, scene_recv)
+    lax.fori_loop(1, scene_count, start, 0)
+    choose(scene, 0)
+    place(scene, scene_out[scene])
+    lax.fori_loop(1, scene_count, finish, 0)
+
+
+def collect_kernel(
+    view_count,
+    scene_count,
+    block_count,
+    send,
+    grads,
+    own_grads,
+    expo,
+    scene_out,
+    scene_in,
+    view_out,
+    view_in,
+    scene_send,
+    scene_recv,
+    view_send,
+    view_recv,
+):
+    view, scene = lax.axis_index("view"), lax.axis_index("scene")
+    capacity = send.shape[1]
+    lanes = grads.shape[2]
+    barrier = greet(view_count, scene_count, view, scene)
+    used = capacity * FEATURES
+    spare = scene_out.shape[1] - used - 1
+
+    def pack(peer, unused):
+        parts = [grads[peer * capacity + at, 0:FEATURES] for at in range(capacity)]
+        parts.append(grads[peer * capacity, FEATURES : FEATURES + 1])
+        scene_out[peer] = jnp.concatenate(fill(parts, spare, lanes), axis=0)
+        return unused
+
+    lax.fori_loop(0, scene_count, pack, 0)
+    pl.semaphore_wait(barrier, view_count + scene_count - 2)
+    scene_sems = (scene_send, scene_recv)
+
+    def start(step, unused):
+        scene_copy(scene_out, scene_in, scene_sems, step, view, scene, scene_count).start()
+        return unused
+
+    def add(source, box, sums):
+        sums = list(sums)
+        for at in range(capacity):
+            part = box[at * FEATURES : (at + 1) * FEATURES]
+            home = send[source, at]
+            for block in range(view_count * block_count):
+                sums[block] = sums[block] + jnp.where(home == block, part, 0.0)
+        sums[-1] = sums[-1] + box[used : used + 1]
+        return tuple(sums)
+
+    def finish(step, sums):
+        scene_copy(scene_out, scene_in, scene_sems, step, view, scene, scene_count).wait()
+        source = lax.rem(scene - step + scene_count, scene_count)
+        return add(source, scene_in[source], sums)
+
+    lax.fori_loop(1, scene_count, start, 0)
+    empty = jnp.zeros((FEATURES, lanes), jnp.float32)
+    sums = (empty,) * (view_count * block_count) + (jnp.zeros((1, lanes), jnp.float32),)
+    sums = add(scene, scene_out[scene], sums)
+    sums = lax.fori_loop(1, scene_count, finish, sums)
+    expo[...] = sums[-1]
+    spare = view_out.shape[1] - block_count * FEATURES
+    for target in range(view_count):
+        parts = list(sums[target * block_count : (target + 1) * block_count])
+        view_out[target] = jnp.concatenate(fill(parts, spare, lanes), axis=0)
+    view_sems = (view_send, view_recv)
+    for step in range(1, view_count):
+        view_copy(view_out, view_in, view_sems, step, view, scene, view_count).start()
+    own_grads[view] = view_out[view]
+    for step in range(1, view_count):
+        view_copy(view_out, view_in, view_sems, step, view, scene, view_count).wait()
+        source = lax.rem(view - step + view_count, view_count)
+        own_grads[source] = view_in[source]
+
+
+def unproject_kernel(
+    cameras,
+    own_grads,
+    expo,
+    means,
+    log_scales,
+    rotations,
+    opacity_logits,
+    colour_coefs,
+    grad_means,
+    grad_log_scales,
+    grad_rotations,
+    grad_opacity,
+    grad_colour,
+    grad_expo,
+):
+    view_count = cameras.shape[0]
+    block_count = means.shape[0]
+    cotangent = [
+        jnp.concatenate(
+            [
+                own_grads[view, block * FEATURES + at : block * FEATURES + at + 1]
+                for view in range(view_count)
+                for block in range(block_count)
+            ],
+            axis=0,
+        )
+        for at in range(FEATURES)
+    ]
+    camera = camera_rows(cameras, block_count)
+    pieces = parameter_rows(
+        (means, log_scales, rotations, opacity_logits, colour_coefs), view_count
+    )
+    unproject = jax.vjp(functools.partial(project, camera), *pieces)[1]
+    parts = unproject(cotangent)
+
+    def store(ref, at, value):
+        total = value[0:block_count]
+        for view in range(1, view_count):
+            total = total + value[view * block_count : (view + 1) * block_count]
+        for block in range(block_count):
+            ref[block, at : at + 1] = total[block : block + 1]
+
+    for at in range(3):
+        store(grad_means, at, parts[0][at])
+        store(grad_log_scales, at, parts[1][at])
+    for at in range(4):
+        store(grad_rotations, at, parts[2][at])
+    store(grad_opacity, 0, parts[3])
+    for at in range(48):
+        store(grad_colour, at, parts[4][at])
+    grad_expo[...] = expo[:, 0:12]
 
 
 def local(
@@ -394,58 +682,70 @@
     view_count = lax.axis_size("view")
     scene_count = lax.axis_size("scene")
     own_params = (means, log_scales, rotations, opacity_logits, colour_coefs)
-    per_device = means.shape[0]
-    owned_count = per_device * view_count
-    feature_count = 9
-    lane_count = means.shape[2]
+    block_count, lanes = means.shape[0], means.shape[2]
     capacity = send_list.shape[3]
-    own_proj, unproject = jax.vjp(
-        lambda *pieces: jax.vmap(lambda cam_row: project(pieces, cam_row))(cameras), *own_params
-    )
-    arrived = lax.all_to_all(own_proj, "view", split_axis=0, concat_axis=0, tiled=True)
-    projected = arrived.reshape(owned_count, feature_count, lane_count)
-    send_picks = send_list[0, 0]
-    outgoing = jnp.take(projected, jnp.maximum(send_picks, 0).reshape(-1), axis=0)
-    outgoing = (
-        outgoing.reshape(scene_count, capacity, feature_count, lane_count)
-        * (send_picks >= 0).astype(jnp.float32)[:, :, None, None]
-    )
-    incoming = lax.all_to_all(outgoing, "scene", split_axis=0, concat_axis=0, tiled=True).reshape(
-        scene_count * capacity, feature_count, lane_count
-    )
-    shown_tiles, grad_incoming = render(tile_ids, pair_slots[0], exposure, incoming, target)
-    returned = lax.all_to_all(
-        grad_incoming.reshape(scene_count, capacity, feature_count + 1, lane_count),
-        "scene",
-        split_axis=0,
-        concat_axis=0,
-        tiled=True,
-    )
-    exposure_grad = jnp.sum(returned[:, 0, feature_count, 0:12], axis=0)
-    returned = returned[:, :, 0:feature_count]
-    home_index = jnp.where(send_picks >= 0, send_picks, owned_count).reshape(-1)
-    grad_projected = (
-        jnp.zeros((owned_count, feature_count, lane_count), jnp.float32)
-        .at[home_index]
-        .add(returned.reshape(-1, feature_count, lane_count), mode="drop")
-    )
-    sent_back = lax.all_to_all(
-        grad_projected.reshape(view_count, per_device, feature_count, lane_count),
-        "view",
-        split_axis=0,
-        concat_axis=0,
-        tiled=True,
-    )
-    param_grads = unproject(sent_back)
-    return (
-        shown_tiles,
-        param_grads[0],
-        param_grads[1],
-        param_grads[2],
-        param_grads[3],
-        param_grads[4],
-        exposure_grad[None],
-    )
+    slots = scene_count * capacity
+    send = send_list[0, 0]
+    smem = pl.BlockSpec(memory_space=pltpu.SMEM)
+    vmem = pl.BlockSpec(memory_space=pltpu.VMEM)
+    view_box = (view_count, padded(block_count * FEATURES), lanes)
+    scene_box = (scene_count, padded(capacity * FEATURES + 1), lanes)
+    limit = 32 * 1024 * 1024
+    incoming = pl.pallas_call(
+        functools.partial(spread_kernel, view_count, scene_count),
+        out_shape=jax.ShapeDtypeStruct((slots, FEATURES, lanes), jnp.float32),
+        in_specs=[smem, smem] + [vmem] * 5,
+        out_specs=vmem,
+        scratch_shapes=[
+            pltpu.VMEM(view_box, jnp.float32),
+            pltpu.VMEM(view_box, jnp.float32),
+            pltpu.VMEM((view_count * block_count, FEATURES, lanes), jnp.float32),
+            pltpu.VMEM(scene_box, jnp.float32),
+            pltpu.VMEM(scene_box, jnp.float32),
+            pltpu.SemaphoreType.DMA((view_count,)),
+            pltpu.SemaphoreType.DMA((view_count,)),
+            pltpu.SemaphoreType.DMA((scene_count,)),
+            pltpu.SemaphoreType.DMA((scene_count,)),
+        ],
+        compiler_params=pltpu.CompilerParams(
+            collective_id=0, has_side_effects=True, vmem_limit_bytes=limit
+        ),
+        name="spread",
+    )(cameras, send, *own_params)
+    shown, grads = render(tile_ids, pair_slots[0], exposure, incoming, target)
+    own_grads, expo = pl.pallas_call(
+        functools.partial(collect_kernel, view_count, scene_count, block_count),
+        out_shape=(
+            jax.ShapeDtypeStruct(view_box, jnp.float32),
+            jax.ShapeDtypeStruct((1, lanes), jnp.float32),
+        ),
+        in_specs=[smem, vmem],
+        out_specs=(vmem, vmem),
+        scratch_shapes=[
+            pltpu.VMEM(scene_box, jnp.float32),
+            pltpu.VMEM(scene_box, jnp.float32),
+            pltpu.VMEM(view_box, jnp.float32),
+            pltpu.VMEM(view_box, jnp.float32),
+            pltpu.SemaphoreType.DMA((scene_count,)),
+            pltpu.SemaphoreType.DMA((scene_count,)),
+            pltpu.SemaphoreType.DMA((view_count,)),
+            pltpu.SemaphoreType.DMA((view_count,)),
+        ],
+        compiler_params=pltpu.CompilerParams(
+            collective_id=1, has_side_effects=True, vmem_limit_bytes=limit
+        ),
+        name="collect",
+    )(send, grads)
+    param_grads = pl.pallas_call(
+        unproject_kernel,
+        out_shape=tuple(jax.ShapeDtypeStruct(own.shape, jnp.float32) for own in own_params)
+        + (jax.ShapeDtypeStruct((1, 12), jnp.float32),),
+        in_specs=[smem] + [vmem] * 7,
+        out_specs=(vmem,) * 6,
+        compiler_params=pltpu.CompilerParams(vmem_limit_bytes=limit),
+        name="unproject",
+    )(cameras, own_grads, expo, *own_params)
+    return (shown,) + tuple(param_grads)
 
 
 def solution(mesh):

time: 88.1 us -> 62.4 us (0.71)
  Pallas kernels: 27.4 us -> 55.7 us
  waiting for transfers between devices: 22 us -> 0 us
  starting transfers between devices: 18.2 us -> 0 us
  other arithmetic: 8 us -> 0 us
  local copies, waits for them, and re-layouts: 10.9 us -> 5.51 us
    pallas_call x0 -> x3, Pallas kernels: none -> 27.4 us  [the longest x1 14 us: local(): pl.pallas_call(functools.partial(spread_kernel, view_count, scene_count),...]
    all_to_all x4 -> x0, waiting for transfers between devices: 22 us -> none  [the longest x1 7.79 us: local(): lax.all_to_all(grad_incoming.reshape(scene_count, capacity, feature_count...]
    all_to_all x4 -> x0, starting transfers between devices: 18.2 us -> none  [the longest x1 6.48 us: local(): lax.all_to_all(outgoing, 'scene', split_axis=0, concat_axis=0, tiled=True)]
    mul x13 -> x0, other arithmetic: 2.25 us -> none  [the longest x1 0.81 us: local(): outgoing.reshape(scene_count, capacity, feature_count, lane_count)]
    scatter-add x1 -> x0, other arithmetic: 1.76 us -> none  [local(): grad_projected = jnp.zeros((owned_count, feature_count, lane_count), jnp....]
    reshape x4 -> x0, local copies, waits for them, and re-layouts: 1.53 us -> none  [the longest x1 0.74 us: local(): grad_incoming.reshape(scene_count, capacity, feature_count + 1, lane_count)]
    add_any x10 -> x0, other arithmetic: 1.41 us -> none  [the longest x1 0.6 us: project(): quat_w = rotations[:, 0] + 3.0]
    unnamed x28 -> x26, local copies, waits for them, and re-layouts: 6.51 us -> 5.35 us
  transfers between devices with their start and end apart: 4 -> 0, of which waited for: 4 -> 0; matrix products, arithmetic and copies ran while one was open for 2% -> 0% of each run, Pallas kernels for 0% -> 0%
where the time goes in v2:
time: 62.4 us; the launch traced here: 61.9 us
  Pallas kernels  55.7 us (89%)
  local copies, waits for them, and re-layouts  5.51 us (9%)
  between operations  0.74 us (1%)
    pallas_call x1, Pallas kernels, render(): pl.pallas_call(render_kernel, out_shape=(jax.ShapeDtypeStruct(target.shap...  28.3 us
    pallas_call x1, Pallas kernels, local(): pl.pallas_call(functools.partial(spread_kernel, view_count, scene_count),...  14 us
    pallas_call x1, Pallas kernels, local(): pl.pallas_call(functools.partial(collect_kernel, view_count, scene_count,...  12 us
    unnamed x26, local copies, waits for them, and re-layouts  5.35 us
    pallas_call x1, Pallas kernels, local(): pl.pallas_call(unproject_kernel, out_shape=tuple((jax.ShapeDtypeStruct(ow...  1.35 us

profile of v2, /device:TPU:0, one launch (start us, length us, event | category | flops | bytes accessed | tf_op | source)
XLA Modules:
  0.0 61.9 jit_solution(9784308189214290329)
XLA Ops:
  0.6 0.0 copy-start.6
  0.6 0.7 %copy-done.6 = f32[2,3,128]{2,0,1:T(2,128)S(1)} copy-done((f32[2,3,128]{2,0,1:T(2,128)S(1)}, f32[2,3,128]{2,0,1:T(2,128)}, u32[]{:S(2)}) %copy-start.6) | copy-done | bytes 3096
  1.3 0.0 copy-start.7
  1.3 0.7 %copy-done.7 = f32[2,3,128]{2,0,1:T(2,128)S(1)} copy-done((f32[2,3,128]{2,0,1:T(2,128)S(1)}, f32[2,3,128]{2,0,1:T(2,128)}, u32[]{:S(2)}) %copy-start.7) | copy-done | bytes 3096
  2.0 0.7 %copy-done.9 = s32[1,1,16,2]{2,3,1,0:T(2,128)S(1)} copy-done((s32[1,1,16,2]{2,3,1,0:T(2,128)S(1)}, s32[1,1,16,2]{2,3,1,0:T(2,128)}, u32[]{:S(2)}) %copy-start.9) | copy-done | bytes 152
  2.7 0.1 copy.18.send
  2.8 0.6 copy-done.8
  3.4 0.1 copy.21.slots
  3.5 0.9 %copy.22.target = f32[1,16,3,256]{3,2,1,0:T(4,128)S(1)} copy(f32[1,16,3,256]{3,1,2,0:T(8,128)} %param.18) | data formatting | bytes 98304 | tf_op args[7]
  4.4 0.0 copy-done
  4.4 0.0 copy-done.1
  4.4 0.0 copy-done.2
  4.4 0.0 copy-done.3
  4.4 0.0 copy-start.4
  4.4 0.0 copy-start.5
  4.4 14.0 %spread.1.incoming = f32[32,9,128]{2,1,0:T(8,128)S(1)} custom-call(f32[2,16]{1,0:T(2,128)S(1)} %copy-done.2, s32[16,2]{1,0:T(8,128)S(1)} %copy.18.send, f32[2,3,128]{2,1,0:T(4,128)S(1)} %copy.19.means, f32[2,3,128]{2,1,0:T(4,128)S(1)} %copy.20.log_scales, f32[2,4,128]{2,1,0:T(4,128)S(1)} %copy-done.1, f32[2,1,128]{2,1,0:T(1,128)S(1)} %copy-done.3, ...), custom_call_target="tpu_custom_call" | custom-call | tf_op jit(solution)/shard_map/spread/pallas_call | solution.py:694
  18.4 0.0 copy-done.4
  18.4 0.0 copy-done.5
  18.5 28.3 %render.1 = (f32[1,16,3,256]{3,2,1,0:T(4,128)S(1)}, f32[32,10,128]{2,1,0:T(8,128)S(1)}) custom-call(s32[1,16]{1,0:T(1,128)S(1)} %copy-done.4, s32[16,4]{1,0:T(8,128)S(1)} %copy.21.slots, f32[1,12]{1,0:T(1,128)S(1)} %copy-done.5, f32[32,9,128]{2,1,0:T(8,128)S(1)} %spread.1.incoming, f32[1,16,3,256]{3,2,1,0:T(4,128)S(1)} %copy.22.target), custom_call_target="tpu_custom_call" | custom-call | tf_op jit(solution)/shard_map/render/pallas_call | solution.py:358
  46.7 0.6 %copy.26 = f32[1,16,3,256]{3,1,2,0:T(8,128)} copy(f32[1,16,3,256]{3,2,1,0:T(4,128)S(1)} %get-tuple-element.27) | data formatting | bytes 98304
  47.4 12.0 %collect.1 = (f32[2,24,128]{2,1,0:T(8,128)S(1)}, f32[1,128]{1,0:T(1,128)S(1)}) custom-call(s32[16,2]{1,0:T(8,128)S(1)} %copy.18.send, f32[32,10,128]{2,1,0:T(8,128)S(1)} %get-tuple-element.18.grads), custom_call_target="tpu_custom_call" | custom-call | tf_op jit(solution)/shard_map/collect/pallas_call | solution.py:716
  59.4 1.3 %unproject.1 = (f32[2,3,128]{2,1,0:T(4,128)S(1)}, f32[2,3,128]{2,1,0:T(4,128)S(1)}, f32[2,4,128]{2,1,0:T(4,128)}, f32[2,1,128]{2,1,0:T(1,128)}, f32[2,48,128]{2,1,0:T(8,128)}, /*index=5*/f32[1,12]{1,0:T(1,128)}) custom-call(f32[2,16]{1,0:T(2,128)S(1)} %copy-done.2, f32[2,24,128]{2,1,0:T(8,128)S(1)} %get-tuple-element.19.own_grads, ...), custom_call_target="tpu_custom_call" | custom-call | tf_op jit(solution)/shard_map/unproject/pallas_call | solution.py:739
  60.8 0.6 copy.27
  61.4 0.6 copy.28
  (8 shorter events, 0.0 us)
Async XLA Ops:
  0.6 0.7 %copy-start.6 = (f32[2,3,128]{2,0,1:T(2,128)S(1)}, f32[2,3,128]{2,0,1:T(2,128)}, u32[]{:S(2)}) copy-start(f32[2,3,128]{2,0,1:T(2,128)} %param.11) | copy-start | bytes 9220
  1.3 0.7 %copy-start.7 = (f32[2,3,128]{2,0,1:T(2,128)S(1)}, f32[2,3,128]{2,0,1:T(2,128)}, u32[]{:S(2)}) copy-start(f32[2,3,128]{2,0,1:T(2,128)} %param.12) | copy-start | bytes 9220
  2.0 0.7 %copy-start.9 = (s32[1,1,16,2]{2,3,1,0:T(2,128)S(1)}, s32[1,1,16,2]{2,3,1,0:T(2,128)}, u32[]{:S(2)}) copy-start(s32[1,1,16,2]{2,3,1,0:T(2,128)} %param.20) | copy-start | bytes 388
  2.7 0.7 %copy-start.8 = (s32[1,16,4]{1,2,0:T(4,128)S(1)}, s32[1,16,4]{1,2,0:T(4,128)}, u32[]{:S(2)}) copy-start(s32[1,16,4]{1,2,0:T(4,128)} %param.21) | copy-start | bytes 772
  3.4 0.9 %copy-start = (f32[2,48,128]{2,1,0:T(8,128)S(1)}, f32[2,48,128]{2,1,0:T(8,128)}, u32[]{:S(2)}) copy-start(f32[2,48,128]{2,1,0:T(8,128)} %colour_coefs.3) | copy-start | bytes 147460
  3.4 0.9 %copy-start.1 = (f32[2,4,128]{2,1,0:T(4,128)S(1)}, f32[2,4,128]{2,1,0:T(4,128)}, u32[]{:S(2)}) copy-start(f32[2,4,128]{2,1,0:T(4,128)} %rotations.3) | copy-start | bytes 12292
  3.5 0.9 %copy-start.2 = (f32[2,16]{1,0:T(2,128)S(1)}, f32[2,16]{1,0:T(2,128)}, u32[]{:S(2)}) copy-start(f32[2,16]{1,0:T(2,128)} %cameras.3) | copy-start | bytes 388
  3.5 0.9 %copy-start.3 = (f32[2,1,128]{2,1,0:T(1,128)S(1)}, f32[2,1,128]{2,1,0:T(1,128)}, u32[]{:S(2)}) copy-start(f32[2,1,128]{2,1,0:T(1,128)} %opacity_logits.3) | copy-start | bytes 3076
  4.4 14.0 %copy-start.4 = (s32[1,16]{1,0:T(1,128)S(1)}, s32[1,16]{1,0:T(1,128)}, u32[]{:S(2)}) copy-start(s32[1,16]{1,0:T(1,128)} %tile_ids.1) | copy-start | bytes 196
  4.4 14.0 %copy-start.5 = (f32[1,12]{1,0:T(1,128)S(1)}, f32[1,12]{1,0:T(1,128)}, u32[]{:S(2)}) copy-start(f32[1,12]{1,0:T(1,128)} %exposure.1) | copy-start | bytes 148

commit v3 on v2

--- a/solution.py
+++ b/solution.py
@@ -181,41 +181,62 @@
     before_mat,
     after_mat,
     powers,
+    pixel_side,
 ):
-    tile_count, slot_count = slots.shape
+    slot_count, tile_count = slots.shape
     lanes = incoming.shape[2]
     row_at = lax.broadcasted_iota(jnp.int32, (2 * lanes, 2 * lanes), 0) % lanes
     col_at = lax.broadcasted_iota(jnp.int32, (2 * lanes, 2 * lanes), 1)
     total = col_at >= lanes
     before_mat[...] = jnp.where(total | (row_at < col_at), 1.0, 0.0).astype(jnp.bfloat16)
     after_mat[...] = jnp.where(total | (row_at > col_at), 1.0, 0.0).astype(jnp.bfloat16)
-    power_at = lax.broadcasted_iota(jnp.int32, (8, PIX), 0)
-    pixel_at = lax.broadcasted_iota(jnp.int32, (8, PIX), 1)
-    side_x = (pixel_at % 16).astype(jnp.float32) - 7.5
-    side_y = (pixel_at // 16).astype(jnp.float32) - 7.5
-    picks = [jnp.ones_like(side_x), side_x, side_y, side_x * side_x, side_x * side_y, side_y * side_y]
-    table = jnp.zeros((8, PIX), jnp.float32)
-    for at, pick in enumerate(picks):
-        table = jnp.where(power_at == at, pick, table)
-    powers[...] = table.astype(jnp.bfloat16)
+
+    def monomials(power_at, pixel_at):
+        side_x = (pixel_at % 16).astype(jnp.float32) - 7.5
+        side_y = (pixel_at // 16).astype(jnp.float32) - 7.5
+        one = jnp.ones_like(side_x)
+        picks = [one, side_x, side_y, side_x * side_x, side_x * side_y, side_y * side_y]
+        table = jnp.zeros_like(side_x)
+        for at, pick in enumerate(picks):
+            table = jnp.where(power_at == at, pick, table)
+        return table.astype(jnp.bfloat16)
+
+    powers[...] = monomials(
+        lax.broadcasted_iota(jnp.int32, (8, PIX), 0), lax.broadcasted_iota(jnp.int32, (8, PIX), 1)
+    )
+    part_at = lax.broadcasted_iota(jnp.int32, (PIX, 32), 1)
+    pixel_side[...] = monomials(
+        jnp.where(part_at < 24, part_at % 8, 8), lax.broadcasted_iota(jnp.int32, (PIX, 32), 0)
+    )
     grads[...] = jnp.zeros_like(grads)
     expo_sum[...] = jnp.zeros_like(expo_sum)
     mixing = [
         [exposure[0, 3 * i + j] + (1.0 if i == j else 0.0) for j in range(3)] for i in range(3)
     ]
     offset = [exposure[0, 9 + i] for i in range(3)]
-    local_x = [
-        lax.broadcasted_iota(jnp.int32, (8, lanes), 0).astype(jnp.float32) + (8.0 * half - 7.5)
-        for half in range(2)
-    ]
     zero_rows = jnp.zeros((2, lanes), jnp.float32)
 
     def load(tile, at, centre_x, centre_y):
-        block = incoming[slots[tile, at]]
+        block = incoming[slots[at, tile]]
         rows = [block[i : i + 1] for i in range(FEATURES)]
         rows[0] = rows[0] - centre_x
         rows[1] = rows[1] - centre_y
         return rows, block[6:9]
+
+    def exponent(rows):
+        pos_x, pos_y, con_a, con_b, con_c, opacity = rows[:6]
+        lean_x = con_a * pos_x + con_b * pos_y
+        lean_y = con_b * pos_x + con_c * pos_y
+        base = jnp.log(opacity) - 0.5 * (pos_x * lean_x + pos_y * lean_y)
+        whole = LOG2E * jnp.concatenate(
+            [base, lean_x, lean_y, -0.5 * con_a, -con_b, -0.5 * con_c, zero_rows], axis=0
+        )
+        first = whole.astype(jnp.bfloat16).astype(jnp.float32)
+        rest = whole - first
+        second = rest.astype(jnp.bfloat16).astype(jnp.float32)
+        return jnp.concatenate(
+            [first, second, rest - second, jnp.zeros((8, lanes), jnp.float32)], axis=0
+        ).astype(jnp.bfloat16)
 
     def one_tile(tile, live):
         tile_id = tile_ids[0, tile]
@@ -225,22 +246,11 @@
         shade = None
         for at in range(live):
             rows, colour = load(tile, at, centre_x, centre_y)
-            wide = [jnp.broadcast_to(row, (8, lanes)) for row in rows[:6]]
-            gap_x = [side - wide[0] for side in local_x]
-            scaled_a = wide[2] * (-0.5 * LOG2E)
-            scaled_b = wide[3] * (-LOG2E)
-            scaled_c = wide[4] * (-0.5 * LOG2E)
-            part_x = [scaled_a * gap * gap for gap in gap_x]
-            pieces = []
-            for line in range(PIX // 16):
-                gap_y = (line - 7.5) - wide[1]
-                part_y = scaled_c * gap_y * gap_y
-                slope = scaled_b * gap_y
-                for half in range(2):
-                    pieces.append(
-                        wide[5] * jnp.exp2(part_x[half] + gap_x[half] * slope + part_y)
-                    )
-            alpha = jnp.concatenate(pieces, axis=0)
+            alpha = jnp.exp2(
+                jnp.dot(
+                    pixel_side[...], exponent(rows), preferred_element_type=jnp.float32
+                )
+            )
             log_keep = jnp.log(1.0 - alpha)
             sums = jnp.dot(
                 split_pair(log_keep), before_mat[...], preferred_element_type=jnp.float32
@@ -264,14 +274,14 @@
                 mixed, pair, (((1,), (1,)), ((), ())), preferred_element_type=jnp.float32
             )
             shade = term if at == 0 else shade + term
-        goal = target[0, tile]
         tone = [shade[i : i + 1] + shade[i + 3 : i + 4] for i in range(3)]
         image = [
             mixing[i][0] * tone[0] + mixing[i][1] * tone[1] + mixing[i][2] * tone[2] + offset[i]
             for i in range(3)
         ]
-        shown[0, tile] = jnp.concatenate(image, axis=0)
-        miss = [image[i] - goal[i : i + 1] for i in range(3)]
+        for i in range(3):
+            shown[i, pl.ds(tile, 1)] = image[i]
+        miss = [image[i] - target[i, pl.ds(tile, 1)] for i in range(3)]
         expo_sum[...] += jnp.concatenate(
             [miss[i] * tone[j] for i in range(3) for j in range(3)] + miss, axis=0
         )
@@ -321,7 +331,7 @@
             d_xx = m_xx - pos_x * (m_x + d_x)
             d_xy = m_xy - pos_x * m_y - pos_y * d_x
             d_yy = m_yy - pos_y * (m_y + d_y)
-            grads[slots[tile, at], 0:FEATURES] += jnp.concatenate(
+            grads[slots[at, tile], 0:FEATURES] += jnp.concatenate(
                 [
                     con_a * d_x + con_b * d_y,
                     con_b * d_x + con_c * d_y,
@@ -337,7 +347,7 @@
     def tile_step(tile, unused):
         live = jnp.int32(0)
         for at in range(slot_count):
-            live = live + jnp.where(slots[tile, at] >= 0, 1, 0)
+            live = live + jnp.where(slots[at, tile] >= 0, 1, 0)
         for number in range(1, slot_count + 1):
             pl.when(live == number)(functools.partial(one_tile, tile, number))
         return unused
@@ -351,7 +361,7 @@
 
 
 def render(tile_ids, slots, exposure, incoming, target):
-    slot_count = slots.shape[1]
+    slot_count = slots.shape[0]
     lanes = incoming.shape[2]
     smem = pl.BlockSpec(memory_space=pltpu.SMEM)
     vmem = pl.BlockSpec(memory_space=pltpu.VMEM)
@@ -371,6 +381,7 @@
             pltpu.VMEM((2 * lanes, 2 * lanes), jnp.bfloat16),
             pltpu.VMEM((2 * lanes, 2 * lanes), jnp.bfloat16),
             pltpu.VMEM((8, PIX), jnp.bfloat16),
+            pltpu.VMEM((PIX, 32), jnp.bfloat16),
         ],
         compiler_params=pltpu.CompilerParams(vmem_limit_bytes=32 * 1024 * 1024),
         name="render",
@@ -395,16 +406,19 @@
 
 
 def parameter_rows(refs, view_count):
-    block_count = refs[0].shape[0]
+    block_count = refs[0].shape[1]
 
     def row(ref, at):
         own = [ref[block, at : at + 1] for block in range(block_count)]
         return jnp.concatenate(own * view_count, axis=0)
 
+    def plane(ref, at):
+        return jnp.concatenate([ref[at]] * view_count, axis=0)
+
     means, log_scales, rotations, opacity_logits, colour_coefs = refs
     return (
-        [row(means, at) for at in range(3)],
-        [row(log_scales, at) for at in range(3)],
+        [plane(means, at) for at in range(3)],
+        [plane(log_scales, at) for at in range(3)],
         [row(rotations, at) for at in range(4)],
         row(opacity_logits, 0),
         [row(colour_coefs, at) for at in range(48)],
@@ -484,8 +498,8 @@
     scene_recv,
 ):
     view, scene = lax.axis_index("view"), lax.axis_index("scene")
-    capacity = send.shape[1]
-    block_count, lanes = means.shape[0], means.shape[2]
+    capacity = send.shape[0]
+    block_count, lanes = means.shape[1], means.shape[2]
     barrier = greet(view_count, scene_count, view, scene)
     rows = project(
         camera_rows(cameras, block_count),
@@ -513,7 +527,7 @@
     spare = scene_out.shape[1] - capacity * FEATURES
 
     def choose(peer, unused):
-        parts = [blocks[jnp.maximum(send[peer, at], 0)] for at in range(capacity)]
+        parts = [blocks[jnp.maximum(send[at, peer], 0)] for at in range(capacity)]
         scene_out[peer] = jnp.concatenate(fill(parts, spare, lanes), axis=0)
         return unused
 
@@ -557,7 +571,7 @@
     view_recv,
 ):
     view, scene = lax.axis_index("view"), lax.axis_index("scene")
-    capacity = send.shape[1]
+    capacity = send.shape[0]
     lanes = grads.shape[2]
     barrier = greet(view_count, scene_count, view, scene)
     used = capacity * FEATURES
@@ -581,7 +595,7 @@
         sums = list(sums)
         for at in range(capacity):
             part = box[at * FEATURES : (at + 1) * FEATURES]
-            home = send[source, at]
+            home = send[at, source]
             for block in range(view_count * block_count):
                 sums[block] = sums[block] + jnp.where(home == block, part, 0.0)
         sums[-1] = sums[-1] + box[used : used + 1]
@@ -629,7 +643,7 @@
     grad_expo,
 ):
     view_count = cameras.shape[0]
-    block_count = means.shape[0]
+    block_count = means.shape[1]
     cotangent = [
         jnp.concatenate(
             [
@@ -648,16 +662,20 @@
     unproject = jax.vjp(functools.partial(project, camera), *pieces)[1]
     parts = unproject(cotangent)
 
-    def store(ref, at, value):
+    def over_views(value):
         total = value[0:block_count]
         for view in range(1, view_count):
             total = total + value[view * block_count : (view + 1) * block_count]
+        return total
+
+    def store(ref, at, value):
+        total = over_views(value)
         for block in range(block_count):
             ref[block, at : at + 1] = total[block : block + 1]
 
     for at in range(3):
-        store(grad_means, at, parts[0][at])
-        store(grad_log_scales, at, parts[1][at])
+        grad_means[at] = over_views(parts[0][at])
+        grad_log_scales[at] = over_views(parts[1][at])
     for at in range(4):
         store(grad_rotations, at, parts[2][at])
     store(grad_opacity, 0, parts[3])
@@ -681,11 +699,17 @@
 ):
     view_count = lax.axis_size("view")
     scene_count = lax.axis_size("scene")
-    own_params = (means, log_scales, rotations, opacity_logits, colour_coefs)
+    own_params = (
+        jnp.transpose(means, (1, 0, 2)),
+        jnp.transpose(log_scales, (1, 0, 2)),
+        rotations,
+        opacity_logits,
+        colour_coefs,
+    )
     block_count, lanes = means.shape[0], means.shape[2]
     capacity = send_list.shape[3]
     slots = scene_count * capacity
-    send = send_list[0, 0]
+    send = send_list[0, 0].T
     smem = pl.BlockSpec(memory_space=pltpu.SMEM)
     vmem = pl.BlockSpec(memory_space=pltpu.VMEM)
     view_box = (view_count, padded(block_count * FEATURES), lanes)
@@ -712,7 +736,9 @@
         ),
         name="spread",
     )(cameras, send, *own_params)
-    shown, grads = render(tile_ids, pair_slots[0], exposure, incoming, target)
+    shown, grads = render(
+        tile_ids, pair_slots[0].T, exposure, incoming, jnp.transpose(target[0], (1, 0, 2))
+    )
     own_grads, expo = pl.pallas_call(
         functools.partial(collect_kernel, view_count, scene_count, block_count),
         out_shape=(
@@ -745,7 +771,11 @@
         compiler_params=pltpu.CompilerParams(vmem_limit_bytes=limit),
         name="unproject",
     )(cameras, own_grads, expo, *own_params)
-    return (shown,) + tuple(param_grads)
+    return (
+        jnp.transpose(shown, (1, 0, 2))[None],
+        jnp.transpose(param_grads[0], (1, 0, 2)),
+        jnp.transpose(param_grads[1], (1, 0, 2)),
+    ) + tuple(param_grads[2:])
 
 
 def solution(mesh):

time: 62.4 us -> 66.2 us (1.061)
  Pallas kernels: 55.7 us -> 62.2 us
  local copies, waits for them, and re-layouts: 5.51 us -> 2.88 us
    pallas_call x1, Pallas kernels: 28.3 us -> 33.9 us  [render(): pl.pallas_call(render_kernel, out_shape=(jax.ShapeDtypeStruct(target.shap...]
    unnamed x26 -> x24, local copies, waits for them, and re-layouts: 5.35 us -> 2.88 us
    pallas_call x1, Pallas kernels: 12 us -> 12.9 us  [local(): pl.pallas_call(functools.partial(collect_kernel, view_count, scene_count,...]
where the time goes in v3:
time: 66.2 us; the launch traced here: 65.8 us
  Pallas kernels  62.2 us (94%)
  local copies, waits for them, and re-layouts  2.88 us (4%)
  between operations  0.73 us (1%)
    pallas_call x1, Pallas kernels, render(): pl.pallas_call(render_kernel, out_shape=(jax.ShapeDtypeStruct(target.shap...  33.9 us
    pallas_call x1, Pallas kernels, local(): pl.pallas_call(functools.partial(spread_kernel, view_count, scene_count),...  13.9 us
    pallas_call x1, Pallas kernels, local(): pl.pallas_call(functools.partial(collect_kernel, view_count, scene_count,...  12.9 us
    unnamed x24, local copies, waits for them, and re-layouts  2.88 us
    pallas_call x1, Pallas kernels, local(): pl.pallas_call(unproject_kernel, out_shape=tuple((jax.ShapeDtypeStruct(ow...  1.39 us

profile of v3, /device:TPU:0, one launch (start us, length us, event | category | flops | bytes accessed | tf_op | source)
XLA Modules:
  0.0 65.8 jit_solution(13698238521330311038)
XLA Ops:
  0.6 0.0 copy-start.6
  0.6 0.0 copy-start.7
  0.7 0.0 copy-start.3
  0.7 0.0 copy-start.4
  0.7 0.6 copy-done.6
  1.3 0.0 copy-done.7
  1.3 0.0 copy-done.3
  1.4 0.0 copy-done.4
  1.4 0.0 copy-start
  1.4 0.8 %copy-done = f32[2,48,128]{2,1,0:T(8,128)S(1)} copy-done((f32[2,48,128]{2,1,0:T(8,128)S(1)}, f32[2,48,128]{2,1,0:T(8,128)}, u32[]{:S(2)}) %copy-start) | copy-done | bytes 49176
  2.2 0.0 copy-start.5
  2.2 0.7 %copy-done.5 = f32[2,3,128]{2,0,1:T(2,128)S(1)} copy-done((f32[2,3,128]{2,0,1:T(2,128)S(1)}, f32[2,3,128]{2,0,1:T(2,128)}, u32[]{:S(2)}) %copy-start.5) | copy-done | bytes 3096
  2.9 0.0 copy-start.8
  2.9 0.7 %copy-done.8 = f32[2,1,128]{2,1,0:T(1,128)S(1)} copy-done((f32[2,1,128]{2,1,0:T(1,128)S(1)}, f32[2,1,128]{2,1,0:T(1,128)}, u32[]{:S(2)}) %copy-start.8) | copy-done | bytes 1048
  3.5 0.0 copy-start.2
  3.5 13.9 %spread.1.incoming = f32[32,9,128]{2,1,0:T(8,128)S(1)} custom-call(f32[2,16]{1,0:T(2,128)S(1)} %copy-done.7, s32[2,16]{1,0:T(2,128)S(1)} %bitcast.21, f32[3,2,128]{2,1,0:T(2,128)S(1)} %bitcast.17, f32[3,2,128]{2,1,0:T(2,128)S(1)} %bitcast.19, f32[2,4,128]{2,1,0:T(4,128)S(1)} %copy-done.3, f32[2,1,128]{2,1,0:T(1,128)S(1)} %copy-done.8, f32[2,48,128]{2,1,0:T(8,128)S(1)} %copy-done), custom_call_target="tpu_custom_call" | custom-call | tf_op jit(solution)/shard_map/spread/pallas_call | solution.py:718
  17.5 0.0 copy-done.2
  17.5 0.0 copy-done.9
  17.5 0.0 copy-done.10
  17.5 0.0 copy-done.11
  17.5 33.9 %render.1 = (f32[3,16,256]{2,1,0:T(8,128)}, f32[32,10,128]{2,1,0:T(8,128)S(1)}) custom-call(s32[1,16]{1,0:T(1,128)S(1)} %copy-done.10, s32[4,16]{1,0:T(4,128)S(1)} %bitcast.23, f32[1,12]{1,0:T(1,128)S(1)} %copy-done.11, f32[32,9,128]{2,1,0:T(8,128)S(1)} %spread.1.incoming, f32[3,16,256]{2,1,0:T(8,128)S(1)} %bitcast.16), custom_call_target="tpu_custom_call" | custom-call | tf_op jit(solution)/shard_map/render/pallas_call | solution.py:368
  51.4 12.9 %collect.1 = (f32[2,24,128]{2,1,0:T(8,128)S(1)}, f32[1,128]{1,0:T(1,128)S(1)}) custom-call(s32[2,16]{1,0:T(2,128)S(1)} %bitcast.22, f32[32,10,128]{2,1,0:T(8,128)S(1)} %get-tuple-element.18.grads), custom_call_target="tpu_custom_call" | custom-call | tf_op jit(solution)/shard_map/collect/pallas_call | solution.py:742
  64.4 0.0 copy-done.1
  64.4 1.4 %unproject.1 = (f32[3,2,128]{2,1,0:T(2,128)}, f32[3,2,128]{2,1,0:T(2,128)}, f32[2,4,128]{2,1,0:T(4,128)}, f32[2,1,128]{2,1,0:T(1,128)}, f32[2,48,128]{2,1,0:T(8,128)}, /*index=5*/f32[1,12]{1,0:T(1,128)}) custom-call(f32[2,16]{1,0:T(2,128)S(1)} %copy-done.7, f32[2,24,128]{2,1,0:T(8,128)S(1)} %get-tuple-element.19.own_grads, ...), custom_call_target="tpu_custom_call" | custom-call | tf_op jit(solution)/shard_map/unproject/pallas_call | solution.py:765
  (4 shorter events, 0.0 us)
Async XLA Ops:
  0.6 0.7 %copy-start.6 = (s32[1,1,16,2]{2,3,1,0:T(2,128)S(1)}, s32[1,1,16,2]{2,3,1,0:T(2,128)}, u32[]{:S(2)}) copy-start(s32[1,1,16,2]{2,3,1,0:T(2,128)} %param.20) | copy-start | bytes 388
  0.6 0.7 %copy-start.7 = (f32[2,16]{1,0:T(2,128)S(1)}, f32[2,16]{1,0:T(2,128)}, u32[]{:S(2)}) copy-start(f32[2,16]{1,0:T(2,128)} %cameras.3) | copy-start | bytes 388
  0.7 0.7 %copy-start.3 = (f32[2,4,128]{2,1,0:T(4,128)S(1)}, f32[2,4,128]{2,1,0:T(4,128)}, u32[]{:S(2)}) copy-start(f32[2,4,128]{2,1,0:T(4,128)} %rotations.3) | copy-start | bytes 12292
  0.7 0.7 %copy-start.4 = (f32[2,3,128]{2,0,1:T(2,128)S(1)}, f32[2,3,128]{2,0,1:T(2,128)}, u32[]{:S(2)}) copy-start(f32[2,3,128]{2,0,1:T(2,128)} %param.11) | copy-start | bytes 9220
  1.4 0.8 %copy-start = (f32[2,48,128]{2,1,0:T(8,128)S(1)}, f32[2,48,128]{2,1,0:T(8,128)}, u32[]{:S(2)}) copy-start(f32[2,48,128]{2,1,0:T(8,128)} %colour_coefs.3) | copy-start | bytes 147460
  2.2 0.7 %copy-start.5 = (f32[2,3,128]{2,0,1:T(2,128)S(1)}, f32[2,3,128]{2,0,1:T(2,128)}, u32[]{:S(2)}) copy-start(f32[2,3,128]{2,0,1:T(2,128)} %param.12) | copy-start | bytes 9220
  2.9 0.7 %copy-start.8 = (f32[2,1,128]{2,1,0:T(1,128)S(1)}, f32[2,1,128]{2,1,0:T(1,128)}, u32[]{:S(2)}) copy-start(f32[2,1,128]{2,1,0:T(1,128)} %opacity_logits.3) | copy-start | bytes 3076
  3.5 13.9 %copy-start.2 = (f32[1,16,3,256]{3,1,2,0:T(8,128)S(1)}, f32[1,16,3,256]{3,1,2,0:T(8,128)}, u32[]{:S(2)}) copy-start(f32[1,16,3,256]{3,1,2,0:T(8,128)} %param.18) | copy-start | bytes 147460
  3.5 13.9 %copy-start.9 = (s32[1,16,4]{1,2,0:T(4,128)S(1)}, s32[1,16,4]{1,2,0:T(4,128)}, u32[]{:S(2)}) copy-start(s32[1,16,4]{1,2,0:T(4,128)} %param.21) | copy-start | bytes 772
  3.5 13.9 %copy-start.10 = (s32[1,16]{1,0:T(1,128)S(1)}, s32[1,16]{1,0:T(1,128)}, u32[]{:S(2)}) copy-start(s32[1,16]{1,0:T(1,128)} %tile_ids.1) | copy-start | bytes 196
  3.5 14.0 %copy-start.11 = (f32[1,12]{1,0:T(1,128)S(1)}, f32[1,12]{1,0:T(1,128)}, u32[]{:S(2)}) copy-start(f32[1,12]{1,0:T(1,128)} %exposure.1) | copy-start | bytes 148
  51.4 12.9 %copy-start.1 = (f32[2,48,128]{2,1,0:T(8,128)S(1)}, f32[2,48,128]{2,1,0:T(8,128)}, u32[]{:S(2)}) copy-start(f32[2,48,128]{2,1,0:T(8,128)} %colour_coefs.3) | copy-start | bytes 147460

commit v4 on v3

--- a/solution.py
+++ b/solution.py
@@ -180,8 +180,6 @@
     expo_sum,
     before_mat,
     after_mat,
-    powers,
-    pixel_side,
 ):
     slot_count, tile_count = slots.shape
     lanes = incoming.shape[2]
@@ -190,30 +188,16 @@
     total = col_at >= lanes
     before_mat[...] = jnp.where(total | (row_at < col_at), 1.0, 0.0).astype(jnp.bfloat16)
     after_mat[...] = jnp.where(total | (row_at > col_at), 1.0, 0.0).astype(jnp.bfloat16)
-
-    def monomials(power_at, pixel_at):
-        side_x = (pixel_at % 16).astype(jnp.float32) - 7.5
-        side_y = (pixel_at // 16).astype(jnp.float32) - 7.5
-        one = jnp.ones_like(side_x)
-        picks = [one, side_x, side_y, side_x * side_x, side_x * side_y, side_y * side_y]
-        table = jnp.zeros_like(side_x)
-        for at, pick in enumerate(picks):
-            table = jnp.where(power_at == at, pick, table)
-        return table.astype(jnp.bfloat16)
-
-    powers[...] = monomials(
-        lax.broadcasted_iota(jnp.int32, (8, PIX), 0), lax.broadcasted_iota(jnp.int32, (8, PIX), 1)
-    )
-    part_at = lax.broadcasted_iota(jnp.int32, (PIX, 32), 1)
-    pixel_side[...] = monomials(
-        jnp.where(part_at < 24, part_at % 8, 8), lax.broadcasted_iota(jnp.int32, (PIX, 32), 0)
-    )
     grads[...] = jnp.zeros_like(grads)
     expo_sum[...] = jnp.zeros_like(expo_sum)
     mixing = [
         [exposure[0, 3 * i + j] + (1.0 if i == j else 0.0) for j in range(3)] for i in range(3)
     ]
     offset = [exposure[0, 9 + i] for i in range(3)]
+    local_x = [
+        lax.broadcasted_iota(jnp.int32, (8, lanes), 0).astype(jnp.float32) + (8.0 * half - 7.5)
+        for half in range(2)
+    ]
     zero_rows = jnp.zeros((2, lanes), jnp.float32)
 
     def load(tile, at, centre_x, centre_y):
@@ -223,20 +207,31 @@
         rows[1] = rows[1] - centre_y
         return rows, block[6:9]
 
-    def exponent(rows):
-        pos_x, pos_y, con_a, con_b, con_c, opacity = rows[:6]
-        lean_x = con_a * pos_x + con_b * pos_y
-        lean_y = con_b * pos_x + con_c * pos_y
-        base = jnp.log(opacity) - 0.5 * (pos_x * lean_x + pos_y * lean_y)
-        whole = LOG2E * jnp.concatenate(
-            [base, lean_x, lean_y, -0.5 * con_a, -con_b, -0.5 * con_c, zero_rows], axis=0
-        )
-        first = whole.astype(jnp.bfloat16).astype(jnp.float32)
-        rest = whole - first
-        second = rest.astype(jnp.bfloat16).astype(jnp.float32)
-        return jnp.concatenate(
-            [first, second, rest - second, jnp.zeros((8, lanes), jnp.float32)], axis=0
-        ).astype(jnp.bfloat16)
+    def moments(heat):
+        flat, tilt, bend = [], [], []
+        for half in range(2):
+            sums = None
+            for line in range(PIX // 32):
+                far = PIX // 16 - 1 - line
+                first = heat[16 * line + 8 * half : 16 * line + 8 * half + 8]
+                last = heat[16 * far + 8 * half : 16 * far + 8 * half + 8]
+                both, apart = last + first, last - first
+                side = far - 7.5
+                terms = (both, apart * side, both * (side * side))
+                sums = terms if sums is None else [a + b for a, b in zip(sums, terms)]
+            flat.append(sums[0])
+            tilt.append(sums[1])
+            bend.append(sums[2])
+        slide = [part * side for part, side in zip(flat, local_x)]
+        fields = [
+            flat[0] + flat[1],
+            slide[0] + slide[1],
+            tilt[0] + tilt[1],
+            slide[0] * local_x[0] + slide[1] * local_x[1],
+            tilt[0] * local_x[0] + tilt[1] * local_x[1],
+            bend[0] + bend[1],
+        ]
+        return [jnp.sum(field, axis=0, keepdims=True) for field in fields]
 
     def one_tile(tile, live):
         tile_id = tile_ids[0, tile]
@@ -246,14 +241,26 @@
         shade = None
         for at in range(live):
             rows, colour = load(tile, at, centre_x, centre_y)
-            alpha = jnp.exp2(
-                jnp.dot(
-                    pixel_side[...], exponent(rows), preferred_element_type=jnp.float32
-                )
-            )
+            wide = [jnp.broadcast_to(row, (8, lanes)) for row in rows[:6]]
+            gap_x = [side - wide[0] for side in local_x]
+            scaled_a = wide[2] * (-0.5 * LOG2E)
+            scaled_b = wide[3] * (-LOG2E)
+            scaled_c = wide[4] * (-0.5 * LOG2E)
+            part_x = [scaled_a * gap * gap for gap in gap_x]
+            pieces = []
+            for line in range(PIX // 16):
+                gap_y = (line - 7.5) - wide[1]
+                part_y = scaled_c * gap_y * gap_y
+                slope = scaled_b * gap_y
+                for half in range(2):
+                    pieces.append(
+                        wide[5] * jnp.exp2(part_x[half] + gap_x[half] * slope + part_y)
+                    )
+            alpha = jnp.concatenate(pieces, axis=0)
             log_keep = jnp.log(1.0 - alpha)
+            width = 2 * lanes if at + 1 < live else lanes
             sums = jnp.dot(
-                split_pair(log_keep), before_mat[...], preferred_element_type=jnp.float32
+                split_pair(log_keep), before_mat[:, :width], preferred_element_type=jnp.float32
             )
             inside = sums[:, :lanes]
             if at > 0:
@@ -312,20 +319,21 @@
             ).astype(jnp.bfloat16)
             pull = jnp.dot(back_side, colour_side, preferred_element_type=jnp.float32)
             gain = weight[at] * pull
-            sums = jnp.dot(split_pair(gain), after_mat[...], preferred_element_type=jnp.float32)
+            width = 2 * lanes if at > 0 else lanes
+            sums = jnp.dot(
+                split_pair(gain), after_mat[:, :width], preferred_element_type=jnp.float32
+            )
             behind = sums[:, :lanes]
             if at + 1 < live:
                 behind = behind + carry
             if at > 0:
                 carry = sums[:, lanes:] if at + 1 == live else carry + sums[:, lanes:]
             heat = gain - behind * ratio[at]
-            moments = jnp.dot(powers[...], split_pair(heat), preferred_element_type=jnp.float32)
-            moments = moments[:, :lanes] + moments[:, lanes:]
             tint = jnp.dot(back_left, weight_pair[at], preferred_element_type=jnp.float32)
             tint = tint[:, :lanes] + tint[:, lanes:]
             tint = tint[0:3] + tint[3:6]
             pos_x, pos_y, con_a, con_b, con_c, opacity = rows[:6]
-            m_one, m_x, m_y, m_xx, m_xy, m_yy = [moments[i : i + 1] for i in range(6)]
+            m_one, m_x, m_y, m_xx, m_xy, m_yy = moments(heat)
             d_x = m_x - pos_x * m_one
             d_y = m_y - pos_y * m_one
             d_xx = m_xx - pos_x * (m_x + d_x)
@@ -380,8 +388,6 @@
             pltpu.VMEM((12, PIX), jnp.float32),
             pltpu.VMEM((2 * lanes, 2 * lanes), jnp.bfloat16),
             pltpu.VMEM((2 * lanes, 2 * lanes), jnp.bfloat16),
-            pltpu.VMEM((8, PIX), jnp.bfloat16),
-            pltpu.VMEM((PIX, 32), jnp.bfloat16),
         ],
         compiler_params=pltpu.CompilerParams(vmem_limit_bytes=32 * 1024 * 1024),
         name="render",

time: 66.2 us -> 52 us (0.79)
  Pallas kernels: 62.2 us -> 47.8 us
    pallas_call x1, Pallas kernels: 33.9 us -> 21.1 us  [render(): pl.pallas_call(render_kernel, out_shape=(jax.ShapeDtypeStruct(target.shap...]
    pallas_call x1, Pallas kernels: 12.9 us -> 11.4 us  [local(): pl.pallas_call(functools.partial(collect_kernel, view_count, scene_count,...]
where the time goes in v4:
time: 52 us; the launch traced here: 51.4 us
  Pallas kernels  47.8 us (92%)
  local copies, waits for them, and re-layouts  2.88 us (6%)
  between operations  0.73 us (1%)
    pallas_call x1, Pallas kernels, render(): pl.pallas_call(render_kernel, out_shape=(jax.ShapeDtypeStruct(target.shap...  21.1 us
    pallas_call x1, Pallas kernels, local(): pl.pallas_call(functools.partial(spread_kernel, view_count, scene_count),...  13.9 us
    pallas_call x1, Pallas kernels, local(): pl.pallas_call(functools.partial(collect_kernel, view_count, scene_count,...  11.4 us
    unnamed x24, local copies, waits for them, and re-layouts  2.88 us
    pallas_call x1, Pallas kernels, local(): pl.pallas_call(unproject_kernel, out_shape=tuple((jax.ShapeDtypeStruct(ow...  1.39 us

profile of v4, /device:TPU:0, one launch (start us, length us, event | category | flops | bytes accessed | tf_op | source)
XLA Modules:
  0.0 51.4 jit_solution(3686626776596432758)
XLA Ops:
  0.6 0.0 copy-start.6
  0.6 0.0 copy-start.7
  0.7 0.0 copy-start.3
  0.7 0.0 copy-start.4
  0.7 0.6 %copy-done.6 = s32[1,1,16,2]{2,3,1,0:T(2,128)S(1)} copy-done((s32[1,1,16,2]{2,3,1,0:T(2,128)S(1)}, s32[1,1,16,2]{2,3,1,0:T(2,128)}, u32[]{:S(2)}) %copy-start.6) | copy-done | bytes 152
  1.3 0.0 copy-done.7
  1.3 0.0 copy-done.3
  1.4 0.0 copy-done.4
  1.4 0.0 copy-start
  1.4 0.8 %copy-done = f32[2,48,128]{2,1,0:T(8,128)S(1)} copy-done((f32[2,48,128]{2,1,0:T(8,128)S(1)}, f32[2,48,128]{2,1,0:T(8,128)}, u32[]{:S(2)}) %copy-start) | copy-done | bytes 49176
  2.2 0.0 copy-start.5
  2.2 0.7 %copy-done.5 = f32[2,3,128]{2,0,1:T(2,128)S(1)} copy-done((f32[2,3,128]{2,0,1:T(2,128)S(1)}, f32[2,3,128]{2,0,1:T(2,128)}, u32[]{:S(2)}) %copy-start.5) | copy-done | bytes 3096
  2.9 0.0 copy-start.8
  2.9 0.7 %copy-done.8 = f32[2,1,128]{2,1,0:T(1,128)S(1)} copy-done((f32[2,1,128]{2,1,0:T(1,128)S(1)}, f32[2,1,128]{2,1,0:T(1,128)}, u32[]{:S(2)}) %copy-start.8) | copy-done | bytes 1048
  3.5 0.0 copy-start.2
  3.5 13.9 %spread.1.incoming = f32[32,9,128]{2,1,0:T(8,128)S(1)} custom-call(f32[2,16]{1,0:T(2,128)S(1)} %copy-done.7, s32[2,16]{1,0:T(2,128)S(1)} %bitcast.21, f32[3,2,128]{2,1,0:T(2,128)S(1)} %bitcast.17, f32[3,2,128]{2,1,0:T(2,128)S(1)} %bitcast.19, f32[2,4,128]{2,1,0:T(4,128)S(1)} %copy-done.3, f32[2,1,128]{2,1,0:T(1,128)S(1)} %copy-done.8, f32[2,48,128]{2,1,0:T(8,128)S(1)} %copy-done), custom_call_target="tpu_custom_call" | custom-call | tf_op jit(solution)/shard_map/spread/pallas_call | solution.py:724
  17.5 0.0 copy-done.2
  17.5 0.0 copy-done.9
  17.5 0.0 copy-done.10
  17.5 0.0 copy-done.11
  17.5 21.1 %render.1 = (f32[3,16,256]{2,1,0:T(8,128)}, f32[32,10,128]{2,1,0:T(8,128)S(1)}) custom-call(s32[1,16]{1,0:T(1,128)S(1)} %copy-done.10, s32[4,16]{1,0:T(4,128)S(1)} %bitcast.23, f32[1,12]{1,0:T(1,128)S(1)} %copy-done.11, f32[32,9,128]{2,1,0:T(8,128)S(1)} %spread.1.incoming, f32[3,16,256]{2,1,0:T(8,128)S(1)} %bitcast.16), custom_call_target="tpu_custom_call" | custom-call | tf_op jit(solution)/shard_map/render/pallas_call | solution.py:376
  38.6 11.4 %collect.1 = (f32[2,24,128]{2,1,0:T(8,128)S(1)}, f32[1,128]{1,0:T(1,128)S(1)}) custom-call(s32[2,16]{1,0:T(2,128)S(1)} %bitcast.22, f32[32,10,128]{2,1,0:T(8,128)S(1)} %get-tuple-element.18.grads), custom_call_target="tpu_custom_call" | custom-call | tf_op jit(solution)/shard_map/collect/pallas_call | solution.py:748
  50.0 0.0 copy-done.1
  50.0 1.4 %unproject.1 = (f32[3,2,128]{2,1,0:T(2,128)}, f32[3,2,128]{2,1,0:T(2,128)}, f32[2,4,128]{2,1,0:T(4,128)}, f32[2,1,128]{2,1,0:T(1,128)}, f32[2,48,128]{2,1,0:T(8,128)}, /*index=5*/f32[1,12]{1,0:T(1,128)}) custom-call(f32[2,16]{1,0:T(2,128)S(1)} %copy-done.7, f32[2,24,128]{2,1,0:T(8,128)S(1)} %get-tuple-element.19.own_grads, ...), custom_call_target="tpu_custom_call" | custom-call | tf_op jit(solution)/shard_map/unproject/pallas_call | solution.py:771
  (4 shorter events, 0.0 us)
Async XLA Ops:
  0.6 0.7 %copy-start.6 = (s32[1,1,16,2]{2,3,1,0:T(2,128)S(1)}, s32[1,1,16,2]{2,3,1,0:T(2,128)}, u32[]{:S(2)}) copy-start(s32[1,1,16,2]{2,3,1,0:T(2,128)} %param.20) | copy-start | bytes 388
  0.6 0.7 %copy-start.7 = (f32[2,16]{1,0:T(2,128)S(1)}, f32[2,16]{1,0:T(2,128)}, u32[]{:S(2)}) copy-start(f32[2,16]{1,0:T(2,128)} %cameras.3) | copy-start | bytes 388
  0.7 0.7 %copy-start.3 = (f32[2,4,128]{2,1,0:T(4,128)S(1)}, f32[2,4,128]{2,1,0:T(4,128)}, u32[]{:S(2)}) copy-start(f32[2,4,128]{2,1,0:T(4,128)} %rotations.3) | copy-start | bytes 12292
  0.7 0.7 %copy-start.4 = (f32[2,3,128]{2,0,1:T(2,128)S(1)}, f32[2,3,128]{2,0,1:T(2,128)}, u32[]{:S(2)}) copy-start(f32[2,3,128]{2,0,1:T(2,128)} %param.11) | copy-start | bytes 9220
  1.4 0.8 %copy-start = (f32[2,48,128]{2,1,0:T(8,128)S(1)}, f32[2,48,128]{2,1,0:T(8,128)}, u32[]{:S(2)}) copy-start(f32[2,48,128]{2,1,0:T(8,128)} %colour_coefs.3) | copy-start | bytes 147460
  2.2 0.7 %copy-start.5 = (f32[2,3,128]{2,0,1:T(2,128)S(1)}, f32[2,3,128]{2,0,1:T(2,128)}, u32[]{:S(2)}) copy-start(f32[2,3,128]{2,0,1:T(2,128)} %param.12) | copy-start | bytes 9220
  2.9 0.7 %copy-start.8 = (f32[2,1,128]{2,1,0:T(1,128)S(1)}, f32[2,1,128]{2,1,0:T(1,128)}, u32[]{:S(2)}) copy-start(f32[2,1,128]{2,1,0:T(1,128)} %opacity_logits.3) | copy-start | bytes 3076
  3.5 13.9 %copy-start.2 = (f32[1,16,3,256]{3,1,2,0:T(8,128)S(1)}, f32[1,16,3,256]{3,1,2,0:T(8,128)}, u32[]{:S(2)}) copy-start(f32[1,16,3,256]{3,1,2,0:T(8,128)} %param.18) | copy-start | bytes 147460
  3.5 13.9 %copy-start.9 = (s32[1,16,4]{1,2,0:T(4,128)S(1)}, s32[1,16,4]{1,2,0:T(4,128)}, u32[]{:S(2)}) copy-start(s32[1,16,4]{1,2,0:T(4,128)} %param.21) | copy-start | bytes 772
  3.5 13.9 %copy-start.10 = (s32[1,16]{1,0:T(1,128)S(1)}, s32[1,16]{1,0:T(1,128)}, u32[]{:S(2)}) copy-start(s32[1,16]{1,0:T(1,128)} %tile_ids.1) | copy-start | bytes 196
  3.5 14.0 %copy-start.11 = (f32[1,12]{1,0:T(1,128)S(1)}, f32[1,12]{1,0:T(1,128)}, u32[]{:S(2)}) copy-start(f32[1,12]{1,0:T(1,128)} %exposure.1) | copy-start | bytes 148
  38.6 11.4 %copy-start.1 = (f32[2,48,128]{2,1,0:T(8,128)S(1)}, f32[2,48,128]{2,1,0:T(8,128)}, u32[]{:S(2)}) copy-start(f32[2,48,128]{2,1,0:T(8,128)} %colour_coefs.3) | copy-start | bytes 147460

commit v5 on v4

--- a/solution.py
+++ b/solution.py
@@ -206,6 +206,13 @@
         rows[0] = rows[0] - centre_x
         rows[1] = rows[1] - centre_y
         return rows, block[6:9]
+
+    def colour_side(tile, at):
+        colour = incoming[slots[at, tile]][6:9]
+        high = colour.astype(jnp.bfloat16).astype(jnp.float32)
+        return jnp.concatenate(
+            [high, colour - high, high, jnp.zeros((7, lanes), jnp.float32)], axis=0
+        ).astype(jnp.bfloat16)
 
     def moments(heat):
         flat, tilt, bend = [], [], []
@@ -309,16 +316,17 @@
                 [back_high, back_high, back_low, jnp.zeros((7, PIX), jnp.float32)], axis=0
             )
         ).astype(jnp.bfloat16)
+        pulls = []
+        for first in range(0, live, 2):
+            sides = [colour_side(tile, at) for at in range(first, min(first + 2, live))]
+            both = jnp.dot(
+                back_side, jnp.concatenate(sides, axis=1), preferred_element_type=jnp.float32
+            )
+            pulls += [both[:, at * lanes : (at + 1) * lanes] for at in range(len(sides))]
         carry = None
         for at in reversed(range(live)):
             rows, colour = load(tile, at, centre_x, centre_y)
-            high = colour.astype(jnp.bfloat16).astype(jnp.float32)
-            low = colour - high
-            colour_side = jnp.concatenate(
-                [high, low, high, jnp.zeros((7, lanes), jnp.float32)], axis=0
-            ).astype(jnp.bfloat16)
-            pull = jnp.dot(back_side, colour_side, preferred_element_type=jnp.float32)
-            gain = weight[at] * pull
+            gain = weight[at] * pulls[at]
             width = 2 * lanes if at > 0 else lanes
             sums = jnp.dot(
                 split_pair(gain), after_mat[:, :width], preferred_element_type=jnp.float32

time: 52 us -> 50 us (0.962)
  Pallas kernels: 47.8 us -> 46.1 us
    pallas_call x1, Pallas kernels: 21.1 us -> 16.8 us  [render(): pl.pallas_call(render_kernel, out_shape=(jax.ShapeDtypeStruct(target.shap...]
    pallas_call x1, Pallas kernels: 11.4 us -> 14 us  [local(): pl.pallas_call(functools.partial(collect_kernel, view_count, scene_count,...]
where the time goes in v5:
time: 50 us; the launch traced here: 49.7 us
  Pallas kernels  46.1 us (92%)
  local copies, waits for them, and re-layouts  2.88 us (6%)
  between operations  0.73 us (1%)
    pallas_call x1, Pallas kernels, render(): pl.pallas_call(render_kernel, out_shape=(jax.ShapeDtypeStruct(target.shap...  16.8 us
    pallas_call x1, Pallas kernels, local(): pl.pallas_call(functools.partial(collect_kernel, view_count, scene_count,...  14 us
    pallas_call x1, Pallas kernels, local(): pl.pallas_call(functools.partial(spread_kernel, view_count, scene_count),...  13.9 us
    unnamed x24, local copies, waits for them, and re-layouts  2.88 us
    pallas_call x1, Pallas kernels, local(): pl.pallas_call(unproject_kernel, out_shape=tuple((jax.ShapeDtypeStruct(ow...  1.39 us

profile of v5, /device:TPU:0, one launch (start us, length us, event | category | flops | bytes accessed | tf_op | source)
XLA Modules:
  0.0 49.7 jit_solution(2251856213699523565)
XLA Ops:
  0.6 0.0 copy-start.6
  0.6 0.0 copy-start.7
  0.7 0.0 copy-start.3
  0.7 0.0 copy-start.4
  0.7 0.6 %copy-done.6 = s32[1,1,16,2]{2,3,1,0:T(2,128)S(1)} copy-done((s32[1,1,16,2]{2,3,1,0:T(2,128)S(1)}, s32[1,1,16,2]{2,3,1,0:T(2,128)}, u32[]{:S(2)}) %copy-start.6) | copy-done | bytes 152
  1.3 0.0 copy-done.7
  1.3 0.0 copy-done.3
  1.4 0.0 copy-done.4
  1.4 0.0 copy-start
  1.4 0.8 %copy-done = f32[2,48,128]{2,1,0:T(8,128)S(1)} copy-done((f32[2,48,128]{2,1,0:T(8,128)S(1)}, f32[2,48,128]{2,1,0:T(8,128)}, u32[]{:S(2)}) %copy-start) | copy-done | bytes 49176
  2.2 0.0 copy-start.5
  2.2 0.7 %copy-done.5 = f32[2,3,128]{2,0,1:T(2,128)S(1)} copy-done((f32[2,3,128]{2,0,1:T(2,128)S(1)}, f32[2,3,128]{2,0,1:T(2,128)}, u32[]{:S(2)}) %copy-start.5) | copy-done | bytes 3096
  2.9 0.0 copy-start.8
  2.9 0.7 %copy-done.8 = f32[2,1,128]{2,1,0:T(1,128)S(1)} copy-done((f32[2,1,128]{2,1,0:T(1,128)S(1)}, f32[2,1,128]{2,1,0:T(1,128)}, u32[]{:S(2)}) %copy-start.8) | copy-done | bytes 1048
  3.5 0.0 copy-start.2
  3.5 13.9 %spread.1.incoming = f32[32,9,128]{2,1,0:T(8,128)S(1)} custom-call(f32[2,16]{1,0:T(2,128)S(1)} %copy-done.7, s32[2,16]{1,0:T(2,128)S(1)} %bitcast.21, f32[3,2,128]{2,1,0:T(2,128)S(1)} %bitcast.17, f32[3,2,128]{2,1,0:T(2,128)S(1)} %bitcast.19, f32[2,4,128]{2,1,0:T(4,128)S(1)} %copy-done.3, f32[2,1,128]{2,1,0:T(1,128)S(1)} %copy-done.8, f32[2,48,128]{2,1,0:T(8,128)S(1)} %copy-done), custom_call_target="tpu_custom_call" | custom-call | tf_op jit(solution)/shard_map/spread/pallas_call | solution.py:732
  17.5 0.0 copy-done.2
  17.5 0.0 copy-done.9
  17.5 0.0 copy-done.10
  17.5 0.0 copy-done.11
  17.5 16.8 %render.1 = (f32[3,16,256]{2,1,0:T(8,128)}, f32[32,10,128]{2,1,0:T(8,128)S(1)}) custom-call(s32[1,16]{1,0:T(1,128)S(1)} %copy-done.10, s32[4,16]{1,0:T(4,128)S(1)} %bitcast.23, f32[1,12]{1,0:T(1,128)S(1)} %copy-done.11, f32[32,9,128]{2,1,0:T(8,128)S(1)} %spread.1.incoming, f32[3,16,256]{2,1,0:T(8,128)S(1)} %bitcast.16), custom_call_target="tpu_custom_call" | custom-call | tf_op jit(solution)/shard_map/render/pallas_call | solution.py:384
  34.3 14.0 %collect.1 = (f32[2,24,128]{2,1,0:T(8,128)S(1)}, f32[1,128]{1,0:T(1,128)S(1)}) custom-call(s32[2,16]{1,0:T(2,128)S(1)} %bitcast.22, f32[32,10,128]{2,1,0:T(8,128)S(1)} %get-tuple-element.18.grads), custom_call_target="tpu_custom_call" | custom-call | tf_op jit(solution)/shard_map/collect/pallas_call | solution.py:756
  48.3 0.0 copy-done.1
  48.3 1.4 %unproject.1 = (f32[3,2,128]{2,1,0:T(2,128)}, f32[3,2,128]{2,1,0:T(2,128)}, f32[2,4,128]{2,1,0:T(4,128)}, f32[2,1,128]{2,1,0:T(1,128)}, f32[2,48,128]{2,1,0:T(8,128)}, /*index=5*/f32[1,12]{1,0:T(1,128)}) custom-call(f32[2,16]{1,0:T(2,128)S(1)} %copy-done.7, f32[2,24,128]{2,1,0:T(8,128)S(1)} %get-tuple-element.19.own_grads, ...), custom_call_target="tpu_custom_call" | custom-call | tf_op jit(solution)/shard_map/unproject/pallas_call | solution.py:779
  (4 shorter events, 0.0 us)
Async XLA Ops:
  0.6 0.7 %copy-start.6 = (s32[1,1,16,2]{2,3,1,0:T(2,128)S(1)}, s32[1,1,16,2]{2,3,1,0:T(2,128)}, u32[]{:S(2)}) copy-start(s32[1,1,16,2]{2,3,1,0:T(2,128)} %param.20) | copy-start | bytes 388
  0.6 0.7 %copy-start.7 = (f32[2,16]{1,0:T(2,128)S(1)}, f32[2,16]{1,0:T(2,128)}, u32[]{:S(2)}) copy-start(f32[2,16]{1,0:T(2,128)} %cameras.3) | copy-start | bytes 388
  0.7 0.7 %copy-start.3 = (f32[2,4,128]{2,1,0:T(4,128)S(1)}, f32[2,4,128]{2,1,0:T(4,128)}, u32[]{:S(2)}) copy-start(f32[2,4,128]{2,1,0:T(4,128)} %rotations.3) | copy-start | bytes 12292
  0.7 0.7 %copy-start.4 = (f32[2,3,128]{2,0,1:T(2,128)S(1)}, f32[2,3,128]{2,0,1:T(2,128)}, u32[]{:S(2)}) copy-start(f32[2,3,128]{2,0,1:T(2,128)} %param.11) | copy-start | bytes 9220
  1.4 0.8 %copy-start = (f32[2,48,128]{2,1,0:T(8,128)S(1)}, f32[2,48,128]{2,1,0:T(8,128)}, u32[]{:S(2)}) copy-start(f32[2,48,128]{2,1,0:T(8,128)} %colour_coefs.3) | copy-start | bytes 147460
  2.2 0.7 %copy-start.5 = (f32[2,3,128]{2,0,1:T(2,128)S(1)}, f32[2,3,128]{2,0,1:T(2,128)}, u32[]{:S(2)}) copy-start(f32[2,3,128]{2,0,1:T(2,128)} %param.12) | copy-start | bytes 9220
  2.9 0.7 %copy-start.8 = (f32[2,1,128]{2,1,0:T(1,128)S(1)}, f32[2,1,128]{2,1,0:T(1,128)}, u32[]{:S(2)}) copy-start(f32[2,1,128]{2,1,0:T(1,128)} %opacity_logits.3) | copy-start | bytes 3076
  3.5 13.9 %copy-start.2 = (f32[1,16,3,256]{3,1,2,0:T(8,128)S(1)}, f32[1,16,3,256]{3,1,2,0:T(8,128)}, u32[]{:S(2)}) copy-start(f32[1,16,3,256]{3,1,2,0:T(8,128)} %param.18) | copy-start | bytes 147460
  3.5 13.9 %copy-start.9 = (s32[1,16,4]{1,2,0:T(4,128)S(1)}, s32[1,16,4]{1,2,0:T(4,128)}, u32[]{:S(2)}) copy-start(s32[1,16,4]{1,2,0:T(4,128)} %param.21) | copy-start | bytes 772
  3.5 13.9 %copy-start.10 = (s32[1,16]{1,0:T(1,128)S(1)}, s32[1,16]{1,0:T(1,128)}, u32[]{:S(2)}) copy-start(s32[1,16]{1,0:T(1,128)} %tile_ids.1) | copy-start | bytes 196
  3.5 14.0 %copy-start.11 = (f32[1,12]{1,0:T(1,128)S(1)}, f32[1,12]{1,0:T(1,128)}, u32[]{:S(2)}) copy-start(f32[1,12]{1,0:T(1,128)} %exposure.1) | copy-start | bytes 148
  34.3 14.0 %copy-start.1 = (f32[2,48,128]{2,1,0:T(8,128)S(1)}, f32[2,48,128]{2,1,0:T(8,128)}, u32[]{:S(2)}) copy-start(f32[2,48,128]{2,1,0:T(8,128)} %colour_coefs.3) | copy-start | bytes 147460
